TPU v7x, 32 devices: a whole 2x2x4 slice. The times are simulated.
32 devices in a mesh: clip: 8 (over z, core), row: 4 (over y, x).
Axes of the slice: x: 2, y: 2, z: 4, core: 2. Of those that a mesh axis runs over, the one named last changes fastest.
Arguments:
- inputs: bfloat16 [32768, 384], P(('clip', 'row')), may hold values from -6 to 6
- cotangent: bfloat16 [32768, 384], P(('clip', 'row')), may hold values from -6 to 6
- source_of: int32 [32768], P(('clip', 'row')), may hold values from 0 to 32767, as said below
- split_row: int32 [8], P('clip'), may hold values from 32 to 64, as said below
- qkv_weight: bfloat16 [2, 384, 1152], P(None, 'row'), may hold values from -0.3125 to 0.3125
- qv_bias: bfloat16 [2, 2, 384], P(None, None, 'row'), may hold values from -3 to 3
- proj_weight: bfloat16 [2, 384, 384], P(None, 'row'), may hold values from -1.25 to 1.25
- proj_bias: bfloat16 [2, 384], P(None, 'row'), may hold values from -2 to 2
- fc1_weight: bfloat16 [2, 384, 1536], P(None, 'row'), may hold values from -0.3125 to 0.3125
- fc1_bias: bfloat16 [2, 1536], P(None, 'row'), may hold values from -2 to 2
- fc2_weight: bfloat16 [2, 1536, 384], P(None, 'row'), may hold values from -0.21875 to 0.21875
- fc2_bias: bfloat16 [2, 384], P(None, 'row'), may hold values from -2 to 2
- norm_gain: bfloat16 [2, 2, 384], P(None, None, 'row'), may hold values from 0.25 to 1.75
- norm_bias: bfloat16 [2, 2, 384], P(None, None, 'row'), may hold values from -2 to 2
- rel_table: float32 [2, 225, 16], replicated, may hold values from -3 to 3
Outputs:
- output: bfloat16 [32768, 384], P(('clip', 'row'))
- input_grad: float32 [32768, 384], P(('clip', 'row'))
- qkv_grad: float32 [2, 384, 1152], P(None, 'row')
- qv_bias_grad: float32 [2, 2, 384], P(None, None, 'row')
- proj_grad: float32 [2, 384, 384], P(None, 'row')
- proj_bias_grad: float32 [2, 384], P(None, 'row')
- fc1_grad: float32 [2, 384, 1536], P(None, 'row')
- fc1_bias_grad: float32 [2, 1536], P(None, 'row')
- fc2_grad: float32 [2, 1536, 384], P(None, 'row')
- fc2_bias_grad: float32 [2, 384], P(None, 'row')
- gain_grad: float32 [2, 2, 384], P(None, None, 'row')
- norm_bias_grad: float32 [2, 2, 384], P(None, None, 'row')
- table_grad: float32 [2, 225, 16], replicated
Inputs may be any that keep to these rules, and one draw needn't show every extreme that they name: `source_of`: A permutation; the slot-layout rows of the device with index j of clip+row have sources on every device, 32 from each, and on device s these sources are its rows j * 32 to (j + 1) * 32 - 1. `split_row`: each entry is 32 or 64; both values occur in every draw.
All inputs are finite; a program needn't handle non-finite values.
Results may differ from a plain program's by a relative error of at most 0.023.
Values may be sent and summed in bfloat16 or wider, within the bound.
A program may use at most 192 MiB of HBM per device.

v0:
```python
import jax
import jax.numpy as jnp
from jax import lax
from jax.sharding import PartitionSpec as P

WIN = 8
SHIFT = 4
GRID_COLS = 64


EPSILON = 1e-05
MASKED = -1000000000.0
HIGHEST = lax.Precision.HIGHEST
ROOT_HALF = 0.7071067811865476
INV_ROOT_TAU = 0.3989422804014327


def shifted_2(value, axis, steps):
    count = lax.axis_size(axis)
    pairs = [(source, (source + steps) % count) for source in range(count)]
    return lax.ppermute(value, axis, pairs)


def shortened(value):
    return jax.tree.map(lambda a: a.astype(jnp.bfloat16) if a.dtype == jnp.float32 else a, value)


def to_windows(values, grid_rows, grid_cols):
    feature = values.shape[-1]
    shaped = values.reshape(grid_rows // WIN, WIN, grid_cols // WIN, WIN, feature)
    return shaped.transpose(0, 2, 1, 3, 4).reshape(-1, WIN * WIN, feature)


def from_windows(values, grid_rows, grid_cols):
    feature = values.shape[-1]
    shaped = values.reshape(grid_rows // WIN, grid_cols // WIN, WIN, WIN, feature)
    return shaped.transpose(0, 2, 1, 3, 4).reshape(grid_rows * grid_cols, feature)


def offset_table():
    place_ids = jnp.arange(WIN)
    spread = jnp.arange(2 * WIN - 1)
    return (
        place_ids[:, None, None] - place_ids[None, :, None] + WIN - 1 == spread[None, None, :]
    ).astype(jnp.float32)


def window_bias(table_rows, offset):
    head_count = table_rows.shape[1]
    table_cube = table_rows.reshape(2 * WIN - 1, 2 * WIN - 1, head_count)
    partial_rows = jnp.einsum("ika,abh->ikbh", offset, table_cube, precision=HIGHEST)
    full_bias = jnp.einsum("jlb,ikbh->hijkl", offset, partial_rows, precision=HIGHEST)
    return full_bias.reshape(head_count, WIN * WIN, WIN * WIN)


def table_from_bias(bias_grad, offset):
    head_count = bias_grad.shape[0]
    shaped = bias_grad.reshape(head_count, WIN, WIN, WIN, WIN)
    partial_rows = jnp.einsum("jlb,hijkl->ikbh", offset, shaped, precision=HIGHEST)
    table_cube = jnp.einsum("ika,ikbh->abh", offset, partial_rows, precision=HIGHEST)
    return table_cube.reshape(-1, head_count)


def norm_forward(values, gain_row, shift_row):
    centred = values - jnp.mean(values, axis=-1, keepdims=True)
    inverse_std = lax.rsqrt(jnp.mean(centred * centred, axis=-1, keepdims=True) + EPSILON)
    normal_part = centred * inverse_std
    return (normal_part * gain_row + shift_row, normal_part, inverse_std)


def norm_backward(upstream, normal_part, inverse_std, gain_row):
    scaled = upstream * gain_row
    centred = scaled - jnp.mean(scaled, axis=-1, keepdims=True)
    values_grad = inverse_std * (
        centred - normal_part * jnp.mean(scaled * normal_part, axis=-1, keepdims=True)
    )
    return (values_grad, jnp.sum(upstream * normal_part, axis=0), jnp.sum(upstream, axis=0))


def window_scores(query_win, key_win, bias_full, same_region):
    score_scale = query_win.shape[-1] ** (-0.5)
    raw_scores = jnp.einsum(
        "wihd,wjhd->whij", query_win, key_win, preferred_element_type=jnp.float32
    )
    return jnp.where(same_region[:, None], raw_scores * score_scale + bias_full[None], MASKED)


def plain_region(first_row, grid_rows, split_at):
    row_ids = first_row + jnp.arange(grid_rows, dtype=jnp.int32)
    upper_clip = (row_ids >= split_at).astype(jnp.int32)
    return jnp.broadcast_to(upper_clip[:, None], (grid_rows, GRID_COLS)).reshape(-1)


def rolled_region(first_row, grid_rows, slot_rows, split_at):
    moved_rows = first_row + jnp.arange(grid_rows, dtype=jnp.int32) + SHIFT
    wrapped = (moved_rows >= slot_rows).astype(jnp.int32)
    row_part = (moved_rows - slot_rows * wrapped >= split_at).astype(jnp.int32) + 2 * wrapped
    col_wrap = (jnp.arange(GRID_COLS, dtype=jnp.int32) + SHIFT >= GRID_COLS).astype(jnp.int32)
    return (2 * row_part[:, None] + col_wrap[None, :]).reshape(-1)


def roll_cols(values, amount):
    model_width = values.shape[-1]
    shaped = values.reshape(-1, GRID_COLS, model_width)
    return jnp.roll(shaped, amount, axis=1).reshape(-1, model_width)


def layer_forward(resid, weights, region, offset):
    (
        w_qkv,
        bias_qv,
        w_proj,
        bias_proj,
        w_up,
        bias_up,
        w_down,
        bias_down,
        gain_pair,
        shift_pair,
        table_rows,
    ) = weights
    model_width = resid.shape[1]
    grid_rows = resid.shape[0] // GRID_COLS
    head_count = table_rows.shape[1]
    head_dim = model_width // head_count
    normed, normal_one, inverse_one = norm_forward(
        resid, gain_pair[0].astype(jnp.float32), shift_pair[0].astype(jnp.float32)
    )
    hidden_one = normed.astype(jnp.bfloat16)
    projected = jnp.dot(hidden_one, w_qkv, preferred_element_type=jnp.float32)
    queries = (projected[:, :model_width] + bias_qv[0].astype(jnp.float32)).astype(jnp.bfloat16)
    keys_all = projected[:, model_width : 2 * model_width].astype(jnp.bfloat16)
    values_all = (projected[:, 2 * model_width :] + bias_qv[1].astype(jnp.float32)).astype(
        jnp.bfloat16
    )

    def heads_of(values):
        return to_windows(values, grid_rows, GRID_COLS).reshape(-1, WIN * WIN, head_count, head_dim)

    query_win = heads_of(queries)
    key_win = heads_of(keys_all)
    value_win = heads_of(values_all)
    bias_full = window_bias(table_rows, offset)
    region_win = to_windows(region[:, None], grid_rows, GRID_COLS)[:, :, 0]
    same_region = region_win[:, :, None] == region_win[:, None, :]
    scores = window_scores(query_win, key_win, bias_full, same_region)
    row_peak = jnp.max(scores, axis=-1, keepdims=True)
    log_total = row_peak + jnp.log(jnp.sum(jnp.exp(scores - row_peak), axis=-1, keepdims=True))
    prob_low = jnp.exp(scores - log_total).astype(jnp.bfloat16)
    mixed_win = jnp.einsum(
        "whij,wjhd->wihd", prob_low, value_win, preferred_element_type=jnp.float32
    )
    attended = from_windows(
        mixed_win.reshape(-1, WIN * WIN, model_width), grid_rows, GRID_COLS
    ).astype(jnp.bfloat16)
    middle = resid + (
        jnp.dot(attended, w_proj, preferred_element_type=jnp.float32)
        + bias_proj.astype(jnp.float32)
    )
    normed_two, normal_two, inverse_two = norm_forward(
        middle, gain_pair[1].astype(jnp.float32), shift_pair[1].astype(jnp.float32)
    )
    hidden_two = normed_two.astype(jnp.bfloat16)
    pre_act = jnp.dot(hidden_two, w_up, preferred_element_type=jnp.float32) + bias_up.astype(
        jnp.float32
    )
    activated = jax.nn.gelu(pre_act, approximate=False).astype(jnp.bfloat16)
    result = middle + (
        jnp.dot(activated, w_down, preferred_element_type=jnp.float32)
        + bias_down.astype(jnp.float32)
    )
    saved_state = (
        normal_one,
        inverse_one,
        hidden_one,
        query_win,
        key_win,
        value_win,
        log_total,
        same_region,
        attended,
        normal_two,
        inverse_two,
        hidden_two,
        pre_act,
        activated,
    )
    return (result, saved_state)


def layer_backward(upstream, saved_state, weights, offset):
    (
        w_qkv,
        bias_qv,
        w_proj,
        bias_proj,
        w_up,
        bias_up,
        w_down,
        bias_down,
        gain_pair,
        shift_pair,
        table_rows,
    ) = weights
    (
        normal_one,
        inverse_one,
        hidden_one,
        query_win,
        key_win,
        value_win,
        log_total,
        same_region,
        attended,
        normal_two,
        inverse_two,
        hidden_two,
        pre_act,
        activated,
    ) = saved_state
    model_width = upstream.shape[1]
    grid_rows = upstream.shape[0] // GRID_COLS
    head_count = table_rows.shape[1]
    head_dim = model_width // head_count
    upstream_low = upstream.astype(jnp.bfloat16)
    down_grad = jnp.einsum("nf,nd->fd", activated, upstream_low, preferred_element_type=jnp.float32)
    down_bias_grad = jnp.sum(upstream_low.astype(jnp.float32), axis=0)
    act_grad = jnp.einsum("nd,fd->nf", upstream_low, w_down, preferred_element_type=jnp.float32)
    slope = (
        0.5 * (1.0 + lax.erf(pre_act * ROOT_HALF))
        + pre_act * jnp.exp(-0.5 * pre_act * pre_act) * INV_ROOT_TAU
    )
    up_grad_low = (act_grad * slope).astype(jnp.bfloat16)
    up_grad = jnp.einsum("nd,nf->df", hidden_two, up_grad_low, preferred_element_type=jnp.float32)
    up_bias_grad = jnp.sum(up_grad_low.astype(jnp.float32), axis=0)
    hidden_two_grad = jnp.einsum("nf,df->nd", up_grad_low, w_up, preferred_element_type=jnp.float32)
    middle_part, gain_two_grad, shift_two_grad = norm_backward(
        hidden_two_grad, normal_two, inverse_two, gain_pair[1].astype(jnp.float32)
    )
    middle_grad = upstream + middle_part
    branch_low = middle_grad.astype(jnp.bfloat16)
    proj_grad = jnp.einsum("nc,nd->cd", attended, branch_low, preferred_element_type=jnp.float32)
    proj_bias_grad = jnp.sum(branch_low.astype(jnp.float32), axis=0)
    attended_grad = jnp.einsum(
        "nd,cd->nc", branch_low, w_proj, preferred_element_type=jnp.float32
    ).astype(jnp.bfloat16)
    mixed_grad = to_windows(attended_grad, grid_rows, GRID_COLS).reshape(
        -1, WIN * WIN, head_count, head_dim
    )
    bias_full = window_bias(table_rows, offset)
    scores = window_scores(query_win, key_win, bias_full, same_region)
    probs = jnp.exp(scores - log_total)
    prob_low = probs.astype(jnp.bfloat16)
    prob_grad = jnp.einsum(
        "wihd,wjhd->whij", mixed_grad, value_win, preferred_element_type=jnp.float32
    )
    value_grad = jnp.einsum(
        "whij,wihd->wjhd", prob_low, mixed_grad, preferred_element_type=jnp.float32
    )
    score_grad = (probs * (prob_grad - jnp.sum(probs * prob_grad, axis=-1, keepdims=True))).astype(
        jnp.bfloat16
    )
    table_part = table_from_bias(jnp.sum(score_grad.astype(jnp.float32), axis=0), offset)
    score_scale = head_dim ** (-0.5)
    query_grad = (
        jnp.einsum("whij,wjhd->wihd", score_grad, key_win, preferred_element_type=jnp.float32)
        * score_scale
    )
    key_grad = (
        jnp.einsum("whij,wihd->wjhd", score_grad, query_win, preferred_element_type=jnp.float32)
        * score_scale
    )
    joined = jnp.concatenate(
        [
            piece_grad.reshape(-1, WIN * WIN, model_width)
            for piece_grad in (query_grad, key_grad, value_grad)
        ],
        axis=-1,
    )
    qkv_grad_low = from_windows(joined, grid_rows, GRID_COLS).astype(jnp.bfloat16)
    qkv_grad = jnp.einsum("nd,ne->de", hidden_one, qkv_grad_low, preferred_element_type=jnp.float32)
    column_sums = jnp.sum(qkv_grad_low.astype(jnp.float32), axis=0)
    qv_bias_grad = jnp.stack([column_sums[:model_width], column_sums[2 * model_width :]])
    hidden_one_grad = jnp.einsum(
        "ne,de->nd", qkv_grad_low, w_qkv, preferred_element_type=jnp.float32
    )
    resid_part, gain_one_grad, shift_one_grad = norm_backward(
        hidden_one_grad, normal_one, inverse_one, gain_pair[0].astype(jnp.float32)
    )
    resid_grad = middle_grad + resid_part
    grads = (
        qkv_grad,
        qv_bias_grad,
        proj_grad,
        proj_bias_grad,
        up_grad,
        up_bias_grad,
        down_grad,
        down_bias_grad,
        jnp.stack([gain_one_grad, gain_two_grad]),
        jnp.stack([shift_one_grad, shift_two_grad]),
        table_part,
    )
    return (resid_grad, grads)


def regroup_in(stacked_rows):
    arrived = lax.all_to_all(stacked_rows, ("clip", "row"), split_axis=1, concat_axis=1, tiled=True)
    return arrived


def regroup_out(out_rows, grad_rows):
    returned = (
        lax.all_to_all(out_rows, ("clip", "row"), split_axis=0, concat_axis=0, tiled=True),
        lax.all_to_all(
            grad_rows.astype(jnp.bfloat16), ("clip", "row"), split_axis=0, concat_axis=0, tiled=True
        ).astype(grad_rows.dtype),
    )
    return returned


def layer_weights(full_weights, layer_index, rel_table):
    return tuple((piece_array[layer_index] for piece_array in full_weights)) + (
        rel_table[layer_index],
    )


def body(
    inputs,
    cotangent,
    source_of,
    split_row,
    qkv_weight,
    qv_bias,
    proj_weight,
    proj_bias,
    fc1_weight,
    fc1_bias,
    fc2_weight,
    fc2_bias,
    norm_gain,
    norm_bias,
    rel_table,
):
    clip_count = lax.axis_size("clip")
    row_count = lax.axis_size("row")
    local_tokens = inputs.shape[0]
    model_width = inputs.shape[1]
    block_rows = local_tokens // (clip_count * row_count)
    grid_rows = local_tokens // GRID_COLS
    slot_rows = grid_rows * row_count
    first_row = lax.axis_index("row") * grid_rows
    placing = source_of // local_tokens * block_rows + source_of % block_rows
    arrived = regroup_in(jnp.stack([inputs, cotangent]))
    start_rows = arrived[0][placing].astype(jnp.float32)
    incoming = arrived[1][placing]
    gathered = (
        lax.all_gather(qkv_weight, "row", axis=1, tiled=True),
        lax.all_gather(qv_bias, "row", axis=2, tiled=True),
        lax.all_gather(proj_weight, "row", axis=1, tiled=True),
        lax.all_gather(proj_bias, "row", axis=1, tiled=True),
        lax.all_gather(fc1_weight, "row", axis=1, tiled=True),
        lax.all_gather(fc1_bias, "row", axis=1, tiled=True),
        lax.all_gather(fc2_weight, "row", axis=1, tiled=True),
        lax.all_gather(fc2_bias, "row", axis=1, tiled=True),
        lax.all_gather(norm_gain, "row", axis=2, tiled=True),
        lax.all_gather(norm_bias, "row", axis=2, tiled=True),
    )
    offset = offset_table()
    split_at = split_row[0]
    region_one = plain_region(first_row, grid_rows, split_at)
    region_two = rolled_region(first_row, grid_rows, slot_rows, split_at)
    layer_one, saved_one = layer_forward(
        start_rows, layer_weights(gathered, 0, rel_table), region_one, offset
    )
    head_rows = SHIFT * GRID_COLS
    ahead_rows = (
        shifted_2(layer_one[:head_rows].astype(jnp.bfloat16), "row", -1).astype(jnp.float32),
        shifted_2(incoming[:head_rows], "row", -1),
    )
    shifted = roll_cols(jnp.concatenate([layer_one[head_rows:], ahead_rows[0]]), -SHIFT)
    shifted_grad = roll_cols(
        jnp.concatenate([incoming[head_rows:], ahead_rows[1]]).astype(jnp.float32), -SHIFT
    )
    layer_two, saved_two = layer_forward(
        shifted, layer_weights(gathered, 1, rel_table), region_two, offset
    )
    grad_two, grads_two = layer_backward(
        shifted_grad, saved_two, layer_weights(gathered, 1, rel_table), offset
    )
    tail_out = roll_cols(layer_two, SHIFT).astype(jnp.bfloat16)
    tail_grad = roll_cols(grad_two, SHIFT)
    behind = shifted_2((tail_out[-head_rows:], shortened(tail_grad[-head_rows:])), "row", 1)
    final_rows = jnp.concatenate([behind[0], tail_out[:-head_rows]])
    grad_into_one = jnp.concatenate([behind[1], tail_grad[:-head_rows]])
    grad_start, grads_one = layer_backward(
        grad_into_one, saved_one, layer_weights(gathered, 0, rel_table), offset
    )
    out_place = jnp.zeros((local_tokens, model_width), jnp.bfloat16).at[placing].set(final_rows)
    grad_place = jnp.zeros((local_tokens, model_width), jnp.float32).at[placing].set(grad_start)
    returned = regroup_out(out_place, grad_place)
    output = returned[0]
    input_grad = returned[1]
    stacked = tuple(
        (
            jnp.stack([grad_first, grad_second])
            for grad_first, grad_second in zip(grads_one, grads_two)
        )
    )
    summed = (
        lax.psum_scatter(
            stacked[0].astype(jnp.bfloat16), "row", scatter_dimension=1, tiled=True
        ).astype(jnp.float32),
        lax.psum_scatter(
            stacked[1].astype(jnp.bfloat16), "row", scatter_dimension=2, tiled=True
        ).astype(jnp.float32),
        lax.psum_scatter(
            stacked[2].astype(jnp.bfloat16), "row", scatter_dimension=1, tiled=True
        ).astype(jnp.float32),
        lax.psum_scatter(
            stacked[3].astype(jnp.bfloat16), "row", scatter_dimension=1, tiled=True
        ).astype(jnp.float32),
        lax.psum_scatter(
            stacked[4].astype(jnp.bfloat16), "row", scatter_dimension=1, tiled=True
        ).astype(jnp.float32),
        lax.psum_scatter(
            stacked[5].astype(jnp.bfloat16), "row", scatter_dimension=1, tiled=True
        ).astype(jnp.float32),
        lax.psum_scatter(
            stacked[6].astype(jnp.bfloat16), "row", scatter_dimension=1, tiled=True
        ).astype(jnp.float32),
        lax.psum_scatter(
            stacked[7].astype(jnp.bfloat16), "row", scatter_dimension=1, tiled=True
        ).astype(jnp.float32),
        lax.psum_scatter(
            stacked[8].astype(jnp.bfloat16), "row", scatter_dimension=2, tiled=True
        ).astype(jnp.float32),
        lax.psum_scatter(
            stacked[9].astype(jnp.bfloat16), "row", scatter_dimension=2, tiled=True
        ).astype(jnp.float32),
    )
    totals = (
        lax.psum(summed[0].astype(jnp.bfloat16), "clip").astype(jnp.float32),
        lax.psum(summed[1].astype(jnp.bfloat16), "clip").astype(jnp.float32),
        lax.psum(summed[2].astype(jnp.bfloat16), "clip").astype(jnp.float32),
        lax.psum(summed[3].astype(jnp.bfloat16), "clip").astype(jnp.float32),
        lax.psum(summed[4].astype(jnp.bfloat16), "clip").astype(jnp.float32),
        lax.psum(summed[5].astype(jnp.bfloat16), "clip").astype(jnp.float32),
        lax.psum(summed[6].astype(jnp.bfloat16), "clip").astype(jnp.float32),
        lax.psum(summed[7].astype(jnp.bfloat16), "clip").astype(jnp.float32),
        lax.psum(summed[8].astype(jnp.bfloat16), "clip").astype(jnp.float32),
        lax.psum(summed[9].astype(jnp.bfloat16), "clip").astype(jnp.float32),
    )
    table_total = lax.psum(stacked[10], ("clip", "row"))
    return (
        output,
        input_grad,
        totals[0],
        totals[1],
        totals[2],
        totals[3],
        totals[4],
        totals[5],
        totals[6],
        totals[7],
        totals[8],
        totals[9],
        table_total,
    )


def solution(mesh):
    placed = (
        P(("clip", "row"), None),
        P(("clip", "row"), None),
        P(("clip", "row")),
        P("clip"),
        P(None, "row", None),
        P(None, None, "row"),
        P(None, "row", None),
        P(None, "row"),
        P(None, "row", None),
        P(None, "row"),
        P(None, "row", None),
        P(None, "row"),
        P(None, None, "row"),
        P(None, None, "row"),
        P(),
    )
    return jax.shard_map(
        body,
        mesh=mesh,
        in_specs=placed,
        out_specs=(
            P(("clip", "row"), None),
            P(("clip", "row"), None),
            P(None, "row", None),
            P(None, None, "row"),
            P(None, "row", None),
            P(None, "row"),
            P(None, "row", None),
            P(None, "row"),
            P(None, "row", None),
            P(None, "row"),
            P(None, None, "row"),
            P(None, None, "row"),
            P(),
        ),
        check_vma=False,
    )
```

profile of v0, /device:TPU:0, one launch (start us, length us, event | category | flops | bytes accessed | tf_op | source)
XLA Modules:
  0.0 898.6 jit_solution(3046161632263804670)
XLA Ops:
  13.0 7.3 all-to-all-start
  21.8 18.9 %all-gather = bf16[4,96,2]{1,2,0:T(2,128)(2,1)S(1)} all-gather(bf16[1,96,2]{1,2,0:T(2,128)(2,1)S(1)} %bitcast.426), channel_id=1, replica_groups=mesh['clip'=8,'row'=4] {'row'}, dimensions={0}, use_global_device_ids=true | all-gather | bytes 1920 | tf_op jit(solution)/shard_map/all_gather | solution.py:361
  40.7 8.4 all-gather.1
  63.9 8.1 all_gather.31
  72.1 9.8 %all_gather.30 = bf16[2,2,384]{1,0,2:T(2,128)(2,1)S(1)} all-gather(bf16[2,2,96]{1,0,2:T(2,128)(2,1)S(1)} %copy.165), channel_id=1, replica_groups=mesh['clip'=8,'row'=4] {'row'}, dimensions={2}, use_global_device_ids=true | all-gather | bytes 3840 | tf_op jit(solution)/shard_map/all_gather | solution.py:366
  81.9 8.0 all_gather.33
  89.9 8.8 all_gather.37
  98.7 10.6 %all_gather.34 = bf16[2,384,384]{2,1,0:T(8,128)(2,1)} all-gather(bf16[2,96,384]{2,1,0:T(8,128)(2,1)S(1)} %copy-done.51), channel_id=1, replica_groups=mesh['clip'=8,'row'=4] {'row'}, dimensions={1}, use_global_device_ids=true | all-gather | bytes 737280 | tf_op jit(solution)/shard_map/all_gather | solution.py:360
  144.7 6.4 reshape_reshape.28
  156.8 6.4 reshape_reshape.26
  168.0 6.4 reshape_reshape.27
  174.4 5.8 copy.171
  196.9 6.0 convert_element_type.454
  204.5 18.3 %fusion.4 = (bf16[1024,1536]{1,0:T(8,128)(2,1)}, f32[1024,1536]{1,0:T(8,128)}) fusion(f32[1536]{0:T(1024)S(1)} %copy-done.88, bf16[2,384,1536]{2,1,0:T(8,128)(2,1)} %all-gather.8.cloned.1.call-done, f32[1024,384]{1,0:T(8,128)S(1)} %get-tuple-element.90, f32[384]{0:T(512)S(1)} %copy-done.71, f32[384]{0:T(512)S(1)} %get-tuple-element.31, ...), kind=kOutput, calls=%fused_computation.24 | convolution fusion | flops 1313734656 | bytes 12207104 | tf_op jit(solution)/shard_map/dot_general | solution.py:164
  237.9 6.8 reshape_reshape.31
  250.3 6.4 reshape_reshape.29
  261.6 7.9 reshape_reshape.30
  269.4 5.7 copy.186
  291.3 6.0 convert_element_type.481
  300.0 16.2 %fusion.7 = (bf16[1024,1536]{1,0:T(8,128)(2,1)}, f32[1024,1536]{1,0:T(8,128)S(1)}) fusion(f32[1536]{0:T(1024)S(1)} %copy-done.90, bf16[2,384,1536]{2,1,0:T(8,128)(2,1)S(1)} %copy-done.117, f32[1024,384]{1,0:T(8,128)S(1)} %get-tuple-element.96, f32[384]{0:T(512)S(1)} %copy-done.73, f32[384]{0:T(512)S(1)} %get-tuple-element.29, ...), kind=kOutput, calls=%fused_computation.27 | convolution fusion | flops 1313734656 | bytes 12210176 | tf_op jit(solution)/shard_map/dot_general | solution.py:164
  327.3 7.6 reshape_reshape.32
  340.6 7.4 fusion.64
  348.0 6.0 multiply_reduce_fusion.1
  369.9 6.8 concatenate.56
  382.2 6.8 concatenate.54
  396.8 6.9 concatenate.55
  433.9 6.4 reshape_reshape.33
  446.0 7.5 convolution_bitcast_fusion
  453.4 9.0 %multiply_reduce_fusion = (f32[16,16,64]{2,1,0:T(8,128)S(1)}, f32[16,16,64,64]{2,3,1,0:T(8,128)}) fusion(f32[16,16,64,64]{2,3,1,0:T(8,128)} %copy-done, f32[16,16,64]{2,1,0:T(8,128)S(1)} %copy-done.35, bf16[16,64,16,24]{1,3,2,0:T(8,128)(2,1)S(1)} %copy-done.17, bf16[16,64,16,24]{1,3,2,0:T(8,128)(2,1)S(1)} %copy-done.13), kind=kOutput, calls=%fused_computation.11 | convolution fusion | flops 53460992 | bytes 10092544 | tf_op jit(solution)/shard_map/wihd,wjhd->whij/dot_general | solution.py:254
  463.4 6.0 copy.221
  469.4 6.0 concatenate.62
  475.4 8.5 convert_reduce_fusion.1
  493.9 6.0 concatenate.60
  499.8 6.1 multiply_bitcast_fusion
  511.5 6.9 concatenate.61
  553.0 5.9 collective-permute-done.1
  558.9 6.6 scatter_custom_fusion
  577.1 7.1 scatter_custom_fusion.1
  602.9 11.0 %reduce-scatter.29.cloned.1.call-done = bf16[2,384,384]{2,1,0:T(8,128)(2,1)} async-done(((bf16[2,1536,384]{2,1,0:T(8,128)(2,1)}), bf16[2,384,384]{2,1,0:T(8,128)(2,1)}) %reduce-scatter.29.cloned.1.call-update) | async-done | bytes 589840 | tf_op jit(solution)/shard_map/reduce_scatter | solution.py:429
  613.9 40.6 %reduce-scatter.27.cloned.1.call-done = bf16[2,96,1536]{2,1,0:T(8,128)(2,1)} async-done(((bf16[2,384,1536]{2,1,0:T(8,128)(2,1)}), bf16[2,96,1536]{2,1,0:T(8,128)(2,1)}) %reduce-scatter.27.cloned.1.call-update) | async-done | bytes 589840 | tf_op jit(solution)/shard_map/reduce_scatter | solution.py:423
  662.2 40.0 %psum.87 = f32[2,225,16]{1,2,0:T(8,128)} all-reduce(f32[2,225,16]{1,2,0:T(8,128)S(1)} %pad_maximum_fusion.13), channel_id=1, replica_groups=mesh['clip'=8,'row'=4] {'clip','row'}, use_global_device_ids=true, to_apply=%region_62.63 | all-reduce | flops 7200 | bytes 57600 | tf_op jit(solution)/shard_map/psum | solution.py:454
  703.1 5.9 reduce-scatter.33.cloned.1.call-done
  709.8 26.4 %reduce-scatter.31.cloned.1.call-done = bf16[96,4]{1,0:T(8,128)(2,1)} async-done(((bf16[384,4]{1,0:T(8,128)(2,1)}), bf16[96,4]{1,0:T(8,128)(2,1)}) %reduce-scatter.31.cloned.1.call-update) | async-done | bytes 784
  737.1 25.6 %reduce-scatter.41.cloned.1.call-done = bf16[96,4]{1,0:T(8,128)(2,1)} async-done(((bf16[384,4]{1,0:T(8,128)(2,1)}), bf16[96,4]{1,0:T(8,128)(2,1)}) %reduce-scatter.41.cloned.1.call-update) | async-done | bytes 784
  763.7 26.3 %reduce-scatter.39.cloned.1.call-done = bf16[96,4]{1,0:T(8,128)(2,1)} async-done(((bf16[384,4]{1,0:T(8,128)(2,1)}), bf16[96,4]{1,0:T(8,128)(2,1)}) %reduce-scatter.39.cloned.1.call-update) | async-done | bytes 784
  790.9 26.9 %reduce-scatter.35.cloned.1.call-done = bf16[384,2]{1,0:T(8,128)(2,1)} async-done(((bf16[1536,2]{1,0:T(8,128)(2,1)}), bf16[384,2]{1,0:T(8,128)(2,1)}) %reduce-scatter.35.cloned.1.call-update) | async-done | bytes 1552
  818.8 16.7 %all-reduce = (bf16[2,2,96]{2,1,0:T(2,128)(2,1)S(1)}, bf16[2,96]{1,0:T(2,128)(2,1)S(1)}, bf16[2,384]{1,0:T(2,128)(2,1)S(1)}, bf16[2,96]{1,0:T(2,128)(2,1)S(1)}, ...) all-reduce(bf16[2,2,96]{2,1,0:T(2,128)(2,1)S(1)} %copy.258, ...), channel_id=1, replica_groups=mesh['clip'=8,'row'=4] {'clip'}, use_global_device_ids=true, to_apply=%region_29.30 | all-reduce | flops 2304 | bytes 9216 | tf_op jit(solution)/shard_map/psum | solution.py:444
  841.4 42.4 %all-reduce.4.cloned.1.call-done = (bf16[2,96,1152]{2,1,0:T(8,128)(2,1)}, bf16[2,96,384]{2,1,0:T(8,128)(2,1)}, bf16[2,96,1536]{2,1,0:T(8,128)(2,1)}, bf16[2,384,384]{2,1,0:T(8,128)(2,1)}) async-done(((bf16[2,96,1152]{2,1,0:T(8,128)(2,1)}, bf16[2,96,384]{2,1,0:T(8,128)(2,1)}, bf16[2,96,1536]{2,1,0:T(8,128)(2,1)}, bf16[2,384,384]{2,1,0:T(8,128)(2,1)}), (bf16[2,96,1152]{2,1,0:T(8,128)(2,1)}, ...) | async-done | bytes 1769488 | tf_op jit(solution)/shard_map/psum | solution.py:443
  (532 shorter events, 317.8 us)
Async XLA Ops:
  7.2 133.9 %all-gather.6.cloned.1.call-start = ((), (), s32[]{:S(2)}) async-start(), calls=%async_computation.13 | async-start | bytes 2211840 | tf_op jit(solution)/shard_map/all_gather | solution.py:358
  7.9 196.5 %all-gather.8.cloned.1.call-start = ((), (), s32[]{:S(2)}) async-start(), calls=%async_computation.14 | async-start | bytes 2949120 | tf_op jit(solution)/shard_map/all_gather | solution.py:362
  13.0 27.8 %copy-start.114 = (bf16[2,96]{1,0:T(2,128)(2,1)S(1)}, bf16[2,96]{1,0:T(2,128)(2,1)}, u32[]{:S(2)}) copy-start(bf16[2,96]{1,0:T(2,128)(2,1)} %param.26) | copy-start | bytes 1156
  13.0 36.2 %copy-start.104 = (bf16[2,2,96]{2,1,0:T(2,128)(2,1)S(1)}, bf16[2,2,96]{2,1,0:T(2,128)(2,1)}, u32[]{:S(2)}) copy-start(bf16[2,2,96]{2,1,0:T(2,128)(2,1)} %param.20) | copy-start | bytes 2308
  13.0 36.4 %copy-start.105 = (bf16[2,2,96]{2,1,0:T(2,128)(2,1)S(1)}, bf16[2,2,96]{2,1,0:T(2,128)(2,1)}, u32[]{:S(2)}) copy-start(bf16[2,2,96]{2,1,0:T(2,128)(2,1)} %param.27) | copy-start | bytes 2308
  13.0 36.5 %copy-start.106 = (bf16[2,2,96]{2,1,0:T(2,128)(2,1)S(1)}, bf16[2,2,96]{2,1,0:T(2,128)(2,1)}, u32[]{:S(2)}) copy-start(bf16[2,2,96]{2,1,0:T(2,128)(2,1)} %param.28) | copy-start | bytes 2308
  13.0 37.0 %copy-start.75 = (f32[2,225,16]{1,2,0:T(8,128)S(1)}, f32[2,225,16]{1,2,0:T(8,128)}, u32[]{:S(2)}) copy-start(f32[2,225,16]{1,2,0:T(8,128)} %param.29) | copy-start | bytes 86404
  13.0 115.1 %all-to-all-start = ((bf16[2,1024,384]{2,0,1:T(2,128)(2,1)}), bf16[2,1024,384]{2,0,1:T(2,128)(2,1)S(1)}, u32[]{:S(2)}, u32[]{:S(2)}) async-start(bf16[2,1024,384]{2,0,1:T(2,128)(2,1)} %copy.163), calls=%async_computation | async-start | bytes 3145728 | tf_op jit(solution)/shard_map/all_to_all | solution.py:308
  20.3 202.5 %all-gather.10.cloned.1.call-start = ((), (), s32[]{:S(2)}) async-start(), calls=%async_computation.15 | async-start | bytes 2949120 | tf_op jit(solution)/shard_map/all_gather | solution.py:364
  21.1 581.8 %reduce-scatter.25.cloned.1.call-start = ((), (), s32[]{:S(2)}) async-start(), calls=%async_computation.17 | async-start | bytes 737280 | tf_op jit(solution)/shard_map/reduce_scatter | solution.py:417
  60.3 29.6 %copy-start.103 = (bf16[2,384]{1,0:T(2,128)(2,1)S(1)}, bf16[2,384]{1,0:T(2,128)(2,1)}, u32[]{:S(2)}) copy-start(bf16[2,384]{1,0:T(2,128)(2,1)} %param.24) | copy-start | bytes 4612
  60.3 38.4 %copy-start.51 = (bf16[2,96,384]{2,1,0:T(8,128)(2,1)S(1)}, bf16[2,96,384]{2,1,0:T(8,128)(2,1)}, u32[]{:S(2)}) copy-start(bf16[2,96,384]{2,1,0:T(8,128)(2,1)} %param.21) | copy-start | bytes 442372
  63.9 61.8 %copy-start.96 = (s32[1024]{0:T(1024)S(1)}, s32[1024]{0:T(1024)}, u32[]{:S(2)}) copy-start(s32[1024]{0:T(1024)} %param.17) | copy-start | bytes 12292
  120.4 20.7 %copy-start.68 = (f32[384]{0:T(512)}, f32[384]{0:T(512)S(1)}, u32[]{:S(2)}) copy-start(f32[384]{0:T(512)S(1)} %get-tuple-element.32) | copy-start | bytes 4612
  120.4 84.0 %copy-start.65 = (f32[384]{0:T(512)}, f32[384]{0:T(512)S(1)}, u32[]{:S(2)}) copy-start(f32[384]{0:T(512)S(1)} %get-tuple-element.31) | copy-start | bytes 4612
  120.4 203.7 %copy-start.63 = (f32[384]{0:T(512)}, f32[384]{0:T(512)S(1)}, u32[]{:S(2)}) copy-start(f32[384]{0:T(512)S(1)} %get-tuple-element.29) | copy-start | bytes 4612
  134.8 93.2 %collective-permute-start.2 = (bf16[256,384]{1,0:T(8,128)(2,1)S(1)}, bf16[256,384]{1,0:T(8,128)(2,1)S(1)}, u32[]{:S(2)}, u32[]{:S(2)}) collective-permute-start(bf16[256,384]{1,0:T(8,128)(2,1)S(1)} %slice.342), channel_id=1, source_target_pairs={{0,3},{1,0},{2,1},{3,2},{4,7},{5,4},{6,5},{7,6},{8,11},{9,8},{10,9... | collective-permute-start | bytes 589832 | tf_op jit(solution)/shard_map/ppermute | solution.py:21
  140.4 62.7 %copy-start.3 = (bf16[1024,384]{1,0:T(8,128)(2,1)}, bf16[1024,384]{1,0:T(8,128)(2,1)S(1)}, u32[]{:S(2)}) copy-start(bf16[1024,384]{1,0:T(8,128)(2,1)S(1)} %gather_fusion) | copy-start | bytes 2359300
  168.0 19.4 %copy-start.12 = (bf16[16,64,16,24]{1,3,2,0:T(8,128)(2,1)}, bf16[16,64,16,24]{1,3,2,0:T(8,128)(2,1)S(1)}, u32[]{:S(2)}) copy-start(bf16[16,64,16,24]{1,3,2,0:T(8,128)(2,1)S(1)} %copy.177) | copy-start | bytes 2359300
  204.0 18.8 %copy-start.5 = (f32[1024,384]{1,0:T(8,128)}, f32[1024,384]{1,0:T(8,128)S(1)}, u32[]{:S(2)}) copy-start(f32[1024,384]{1,0:T(8,128)S(1)} %get-tuple-element.90) | copy-start | bytes 4718596
  204.0 18.8 %copy-start.54 = (f32[1024]{0:T(1024)}, f32[1024]{0:T(1024)S(1)}, u32[]{:S(2)}) copy-start(f32[1024]{0:T(1024)S(1)} %broadcast_multiply_fusion.10) | copy-start | bytes 12292
  204.4 18.4 %copy-start.60 = (f32[1024]{0:T(1024)}, f32[1024]{0:T(1024)S(1)}, u32[]{:S(2)}) copy-start(f32[1024]{0:T(1024)S(1)} %add_rsqrt_fusion.2) | copy-start | bytes 12292
  204.5 18.4 %copy-start.102 = (f32[384]{0:T(512)S(1)}, f32[384]{0:T(512)}, u32[]{:S(2)}) copy-start(f32[384]{0:T(512)} %get-tuple-element.44) | copy-start | bytes 4612
  227.0 5.7 collective-permute-start
  261.6 20.7 %copy-start.14 = (bf16[16,64,16,24]{1,3,2,0:T(8,128)(2,1)}, bf16[16,64,16,24]{1,3,2,0:T(8,128)(2,1)S(1)}, u32[]{:S(2)}) copy-start(bf16[16,64,16,24]{1,3,2,0:T(8,128)(2,1)S(1)} %copy.192) | copy-start | bytes 2359300
  298.3 25.8 %copy-start.7 = (f32[1024,384]{1,0:T(8,128)}, f32[1024,384]{1,0:T(8,128)S(1)}, u32[]{:S(2)}) copy-start(f32[1024,384]{1,0:T(8,128)S(1)} %get-tuple-element.96) | copy-start | bytes 4718596
  298.7 25.4 %copy-start.58 = (f32[1024]{0:T(1024)}, f32[1024]{0:T(1024)S(1)}, u32[]{:S(2)}) copy-start(f32[1024]{0:T(1024)S(1)} %add_rsqrt_fusion.1) | copy-start | bytes 12292
  300.0 16.2 %copy-start.115 = (bf16[2,1536,384]{2,1,0:T(8,128)(2,1)S(1)}, bf16[2,1536,384]{2,1,0:T(8,128)(2,1)}, u32[]{:S(2)}) copy-start(bf16[2,1536,384]{2,1,0:T(8,128)(2,1)} %all-gather.10.cloned.1.call-done) | copy-start | bytes 7077892
  416.0 6.6 collective-permute-start.3
  463.4 139.5 %reduce-scatter.23.cloned.1.call-start = ((), (), s32[]{:S(2)}) async-start(), calls=%async_computation.16 | async-start | bytes 2211840 | tf_op jit(solution)/shard_map/reduce_scatter | solution.py:411
  525.6 88.3 %reduce-scatter.29.cloned.1.call-start = ((), (), s32[]{:S(2)}) async-start(), calls=%async_computation.19 | async-start | bytes 2949120 | tf_op jit(solution)/shard_map/reduce_scatter | solution.py:429
  534.7 119.8 %reduce-scatter.27.cloned.1.call-start = ((), (), s32[]{:S(2)}) async-start(), calls=%async_computation.18 | async-start | bytes 2949120 | tf_op jit(solution)/shard_map/reduce_scatter | solution.py:423
  548.8 10.1 %collective-permute-start.1 = (bf16[256,384]{1,0:T(8,128)(2,1)S(1)}, bf16[256,384]{1,0:T(8,128)(2,1)S(1)}, u32[]{:S(2)}, u32[]{:S(2)}) collective-permute-start(bf16[256,384]{1,0:T(8,128)(2,1)S(1)} %bitcast.420), channel_id=1, source_target_pairs={{0,1},{1,2},{2,3},{3,0},{4,5},{5,6},{6,7},{7,4},{8,9},{9,10},{10,1... | collective-permute-start | bytes 589832 | tf_op jit(solution)/shard_map/ppermute | solution.py:21
  551.6 19.0 %copy-start.100 = (bf16[384]{0:T(512)(128)(2,1)S(1)}, bf16[384]{0:T(512)(128)(2,1)}, u32[]{:S(2)}) copy-start(bf16[384]{0:T(512)(128)(2,1)} %get-tuple-element.64) | copy-start | bytes 2308
  551.6 19.0 %copy-start.99 = (bf16[384]{0:T(512)(128)(2,1)S(1)}, bf16[384]{0:T(512)(128)(2,1)}, u32[]{:S(2)}) copy-start(bf16[384]{0:T(512)(128)(2,1)} %get-tuple-element.78) | copy-start | bytes 2308
  551.6 19.0 %copy-start.91 = (bf16[1,384]{1,0:T(2,128)(2,1)S(1)}, bf16[1,384]{1,0:T(2,128)(2,1)}, u32[]{:S(2)}) copy-start(bf16[1,384]{1,0:T(2,128)(2,1)} %stack.235) | copy-start | bytes 2308
  552.8 18.7 %copy-start.80 = (bf16[1152]{0:T(1024)(128)(2,1)S(1)}, bf16[1152]{0:T(1024)(128)(2,1)}, u32[]{:S(2)}) copy-start(bf16[1152]{0:T(1024)(128)(2,1)} %get-tuple-element.76) | copy-start | bytes 6916
  552.8 18.7 %copy-start.70 = (f32[384]{0:T(512)S(1)}, f32[384]{0:T(512)}, u32[]{:S(2)}) copy-start(f32[384]{0:T(512)} %copy-done.68) | copy-start | bytes 4612
  565.5 26.4 %all-to-all-start.1 = ((bf16[32,32,384]{2,1,0:T(8,128)(2,1)}), bf16[32,32,384]{2,1,0:T(8,128)(2,1)S(1)}, u32[]{:S(2)}, u32[]{:S(2)}) async-start(bf16[32,32,384]{2,1,0:T(8,128)(2,1)} %bitcast.57), calls=%async_computation.1 | async-start | bytes 1572864 | tf_op jit(solution)/shard_map/all_to_all | solution.py:314
  570.5 131.8 %reduce-scatter.37.cloned.1.call-start = ((), (), s32[]{:S(2)}) async-start(), calls=%async_computation.23 | async-start | bytes 122880
  571.4 137.6 %reduce-scatter.33.cloned.1.call-start = ((), (), s32[]{:S(2)}) async-start(), calls=%async_computation.21 | async-start | bytes 122880
  591.9 247.1 %all-to-all-start.2 = ((bf16[32,32,384]{2,1,0:T(8,128)(2,1)}), bf16[32,32,384]{2,1,0:T(8,128)(2,1)}, u32[]{:S(2)}, u32[]{:S(2)}) async-start(bf16[32,32,384]{2,1,0:T(8,128)(2,1)} %bitcast.81), calls=%async_computation.2 | async-start | bytes 1572864 | tf_op jit(solution)/shard_map/all_to_all | solution.py:315
  595.2 141.0 %reduce-scatter.31.cloned.1.call-start = ((), (), s32[]{:S(2)}) async-start(), calls=%async_computation.20 | async-start | bytes 122880
  596.3 166.5 %reduce-scatter.41.cloned.1.call-start = ((), (), s32[]{:S(2)}) async-start(), calls=%async_computation.25 | async-start | bytes 122880
  597.4 192.6 %reduce-scatter.39.cloned.1.call-start = ((), (), s32[]{:S(2)}) async-start(), calls=%async_computation.24 | async-start | bytes 122880
  598.6 219.3 %reduce-scatter.35.cloned.1.call-start = ((), (), s32[]{:S(2)}) async-start(), calls=%async_computation.22 | async-start | bytes 491520
  599.6 54.9 %copy-start.48 = (s32[8,8]{1,0:T(8,128)S(1)}, s32[8,8]{1,0:T(8,128)}, u32[]{:S(2)}) copy-start(s32[8,8]{1,0:T(8,128)} %copy-done.47) | copy-start | bytes 772
  599.6 284.1 %all-reduce.4.cloned.1.call-start = ((), (), s32[]{:S(2)}) async-start(), calls=%async_computation.26 | async-start | bytes 3538944 | tf_op jit(solution)/shard_map/psum | solution.py:443
  (98 other events, 450.7 us)
Sparse Core Ops, SparseCore 0:
  9.9 50.9 all-gather.5
  62.7 40.9 all-gather.7
  105.5 41.6 all-gather.9
  463.5 25.0 reduce-scatter.24
  525.7 35.0 reduce-scatter.22
  564.0 49.8 reduce-scatter.28
  617.2 37.2 reduce-scatter.26
  658.0 23.7 reduce-scatter.36
  685.2 23.7 reduce-scatter.32
  712.4 23.8 reduce-scatter.30
  739.0 23.7 reduce-scatter.40
  766.2 23.8 reduce-scatter.38
  793.4 24.4 reduce-scatter.34
  820.3 63.3 all-reduce.3
where the time goes:
time: 909 us; the launch traced here: 899 us
  local copies, waits for them, and re-layouts  261 us (29%)
  waiting for transfers between devices  224 us (25%)
  matrix products  155 us (17%)
  blocking collectives  129 us (14%)
  other arithmetic  90.8 us (10%)
  starting transfers between devices  21 us (2%)
  between operations  17.1 us (2%)
    unnamed x20, waiting for transfers between devices  113 us
    another operation x12, local copies, waits for them, and re-layouts, heads_of(): to_windows(values, grid_rows, GRID_COLS)  72.8 us
    psum x1, waiting for transfers between devices, body(): lax.psum(summed[0].astype(jnp.bfloat16), 'clip').astype(jnp.float32)  42.4 us
    concatenate x7, local copies, waits for them, and re-layouts, layer_backward(): jnp.concatenate([piece_grad.reshape(-1, WIN * WIN, model_width) for piece...  41.5 us
    reduce_scatter x1, waiting for transfers between devices, body(): lax.psum_scatter(stacked[4].astype(jnp.bfloat16), 'row', scatter_dimensio...  40.6 us
    psum x1, blocking collectives, body(): table_total = lax.psum(stacked[10], ('clip', 'row'))  40 us
    dot_general x2, matrix products, layer_forward(): jnp.dot(hidden_two, w_up, preferred_element_type=jnp.float32)  34.5 us
    unnamed x276, local copies, waits for them, and re-layouts  26.4 us
  transfers between devices with their start and end apart: 21, of which 12 were waited for; matrix products, arithmetic and copies ran while one was open for 30% of the time, Pallas kernels for 0%

commit v1 on v0

v1 whole, which is shorter than its diff:
```python
import functools

import jax
import jax.numpy as jnp
import numpy as np
from jax import lax
from jax.experimental import pallas as pl
from jax.experimental.pallas import tpu as pltpu
from jax.sharding import PartitionSpec as P

WIN = 8
SHIFT = 4
GRID_COLS = 64
EPSILON = 1e-05
MASKED = -1000000000.0
ROOT_HALF = 0.7071067811865476
INV_ROOT_TAU = 0.3989422804014327

HEADS = 16
HEAD_DIM = 24
D = HEADS * HEAD_DIM
GROUP = 8
CELL = WIN * WIN
BLOCK = SHIFT * SHIFT
WIN_COLS = GRID_COLS // WIN
SPREAD = 2 * WIN - 1
TABLE = SPREAD * SPREAD
TABLE_PAD = 256
SCALE = HEAD_DIM**-0.5
CHUNK = 256
CHUNK_WINS = CHUNK // CELL
VMEM_LIMIT = 56 * 1024 * 1024

f32 = jnp.float32
bf16 = jnp.bfloat16


def window_places():
    spot = np.arange(CELL)
    row = (spot // 32) * SHIFT + (spot % BLOCK) // SHIFT
    col = (spot // BLOCK % 2) * SHIFT + spot % SHIFT
    return row, col


def head_masks():
    feature = np.arange(D) // HEAD_DIM
    rows = (feature[None, :] == np.arange(HEADS)[:, None]).astype(np.float32)
    wide = np.stack(
        [
            np.repeat(rows[GROUP * g : GROUP * (g + 1), 128 * g : 128 * g + 256], CELL, axis=0)
            for g in range(2)
        ]
    )
    return rows, wide


def table_constants():
    row, col = window_places()
    natural = row * WIN + col
    lanes = np.zeros((2, TABLE_PAD, 128), np.float32)
    for half in range(2):
        lanes[half, row * SPREAD + col, half * CELL + np.arange(CELL)] = 1.0
    order = np.zeros((CELL, CELL), np.float32)
    order[np.arange(CELL), natural] = 1.0
    back = np.zeros((CELL, CELL), np.float32)
    back[row * WIN + (WIN - 1 - col), np.arange(CELL)] = 1.0
    return lanes, order, back


def dot_nn(a, b):
    return lax.dot_general(a, b, (((1,), (0,)), ((), ())), preferred_element_type=f32)


def dot_nt(a, b):
    return lax.dot_general(a, b, (((1,), (1,)), ((), ())), preferred_element_type=f32)


def dot_tn(a, b):
    return lax.dot_general(a, b, (((0,), (0,)), ((), ())), preferred_element_type=f32)


def dot_exact(a, b, dims):
    return lax.dot_general(
        a, b, (dims, ((), ())), precision=lax.Precision.HIGHEST, preferred_element_type=f32
    )


def whole(shape):
    zeros = (0,) * len(shape)
    return pl.BlockSpec(shape, lambda i: zeros)


def rows_of(shape):
    return pl.BlockSpec(shape, lambda i: (i, 0))


def norm_parts(values):
    centred = values - jnp.mean(values, axis=-1, keepdims=True)
    inverse = lax.rsqrt(jnp.mean(centred * centred, axis=-1, keepdims=True) + EPSILON)
    return centred * inverse, inverse


def norm_back(upstream, normal, inverse, gain):
    scaled = upstream * gain
    centred = scaled - jnp.mean(scaled, axis=-1, keepdims=True)
    return inverse * (centred - normal * jnp.mean(scaled * normal, axis=-1, keepdims=True))


def column_sum(values):
    return jnp.sum(values, axis=0, keepdims=True)


def bias_kernel(table_ref, lanes_ref, order_ref, out_ref, wide_ref):
    for layer in range(2):
        for pair in range(HEADS // 2):
            halves = []
            for half in range(2):
                row = table_ref[layer, 2 * pair + half : 2 * pair + half + 1, :]
                spread = jnp.broadcast_to(row, (WIN, TABLE_PAD))
                for i in range(WIN):
                    wide_ref[WIN * i : WIN * (i + 1), :] = pltpu.roll(
                        spread, (SPREAD * i - 112) % TABLE_PAD, 1, stride=1, stride_axis=0
                    )
                halves.append(dot_exact(wide_ref[...], lanes_ref[half], ((1,), (0,))))
            out_ref[layer, :, 128 * pair : 128 * (pair + 1)] = dot_exact(
                order_ref[...], halves[0] + halves[1], ((1,), (0,))
            )


def bias_tables(rel_table):
    lanes, order, _ = table_constants()
    rows = jnp.pad(rel_table.transpose(0, 2, 1), ((0, 0), (0, 0), (0, TABLE_PAD - TABLE)))
    return pl.pallas_call(
        bias_kernel,
        out_shape=jax.ShapeDtypeStruct((2, CELL, HEADS * CELL), f32),
        scratch_shapes=[pltpu.VMEM((CELL, TABLE_PAD), f32)],
        name="bias_tables",
    )(rows, jnp.asarray(lanes), jnp.asarray(order))


def table_kernel(one_ref, two_ref, lanes_ref, back_ref, out_ref):
    for layer, grad_ref in enumerate((one_ref, two_ref)):
        for pair in range(HEADS // 2):
            turned = dot_exact(
                back_ref[...], grad_ref[:, 128 * pair : 128 * (pair + 1)], ((1,), (0,))
            )
            for half in range(2):
                spread = dot_exact(turned, lanes_ref[half], ((1,), (1,)))
                total = jnp.zeros((WIN, TABLE_PAD), f32)
                for i in range(WIN):
                    total += pltpu.roll(
                        spread[WIN * i : WIN * (i + 1), :],
                        (112 - SPREAD * i - (WIN - 1)) % TABLE_PAD,
                        1,
                        stride=1,
                        stride_axis=0,
                    )
                out_ref[layer, 2 * pair + half : 2 * pair + half + 1, :] = column_sum(total)


def table_sums(grad_one, grad_two):
    lanes, _, back = table_constants()
    return pl.pallas_call(
        table_kernel,
        out_shape=jax.ShapeDtypeStruct((2, HEADS, TABLE_PAD), f32),
        name="table_sums",
    )(grad_one, grad_two, jnp.asarray(lanes), jnp.asarray(back))


def place_kernel(place_ref, rows_ref, out_ref):
    spots = lax.broadcasted_iota(jnp.int32, (CHUNK, rows_ref.shape[0]), 1)
    pick = jnp.where(spots == place_ref[...], 1.0, 0.0).astype(bf16)
    out_ref[...] = dot_nn(pick, rows_ref[...]).astype(out_ref.dtype)


def place_rows(place, rows):
    tokens, width = rows.shape
    return pl.pallas_call(
        place_kernel,
        grid=(tokens // CHUNK,),
        in_specs=[rows_of((CHUNK, 1)), whole((tokens, width))],
        out_specs=rows_of((CHUNK, width)),
        out_shape=jax.ShapeDtypeStruct((tokens, width), bf16),
        name="place_rows",
    )(place, rows)


def unplace_kernel(place_ref, main_ref, edge_ref, out_ref, wide_ref):
    step = pl.program_id(0)

    @pl.when(step == 0)
    def _():
        assemble_back(main_ref, edge_ref, wide_ref)

    tokens = main_ref.shape[0]
    spots = lax.broadcasted_iota(jnp.int32, (CHUNK, tokens), 0) + step * CHUNK
    pick = jnp.where(spots == place_ref[...], 1.0, 0.0).astype(bf16)
    out_ref[...] = dot_nn(pick, wide_ref[...]).astype(out_ref.dtype)


def quarter(window, sub):
    return pl.ds(CELL * window + BLOCK * sub, BLOCK)


def assemble_back(main_ref, edge_ref, out_ref):
    windows = main_ref.shape[0] // CELL
    for window in range(windows):
        wr, wc = divmod(window, WIN_COLS)
        before = (wc - 1) % WIN_COLS
        out_ref[quarter(window, 3), :] = main_ref[quarter(window, 0), :].astype(out_ref.dtype)
        out_ref[quarter(window, 2), :] = main_ref[
            quarter(wr * WIN_COLS + before, 1), :
        ].astype(out_ref.dtype)
        for sub, col, piece in ((1, wc, 0), (0, before, 1)):
            if wr == 0:
                value = edge_ref[pl.ds(2 * BLOCK * col + BLOCK * piece, BLOCK), :]
            else:
                value = main_ref[quarter((wr - 1) * WIN_COLS + col, 2 + piece), :]
            out_ref[quarter(window, sub), :] = value.astype(out_ref.dtype)


def assemble_ahead(main_ref, edge_ref, out_ref):
    windows = main_ref.shape[0] // CELL
    last = windows // WIN_COLS - 1
    for window in range(windows):
        wr, wc = divmod(window, WIN_COLS)
        after = (wc + 1) % WIN_COLS
        out_ref[quarter(window, 0), :] = main_ref[quarter(window, 3), :].astype(out_ref.dtype)
        out_ref[quarter(window, 1), :] = main_ref[
            quarter(wr * WIN_COLS + after, 2), :
        ].astype(out_ref.dtype)
        for sub, col, piece in ((2, wc, 1), (3, after, 0)):
            if wr == last:
                value = edge_ref[pl.ds(2 * BLOCK * col + BLOCK * piece, BLOCK), :]
            else:
                value = main_ref[quarter((wr + 1) * WIN_COLS + col, piece), :]
            out_ref[quarter(window, sub), :] = value.astype(out_ref.dtype)


def unplace_rows(place, main, edge):
    tokens, width = main.shape
    return pl.pallas_call(
        unplace_kernel,
        grid=(tokens // CHUNK,),
        in_specs=[whole((1, tokens)), whole((tokens, width)), whole(edge.shape)],
        out_specs=rows_of((CHUNK, width)),
        out_shape=jax.ShapeDtypeStruct((tokens, width), bf16),
        scratch_shapes=[pltpu.VMEM((tokens, width), bf16)],
        name="unplace_rows",
    )(place, main, edge)


def forward_kernel(
    layer,
    mask_ref,
    *refs,
):
    if layer == 0:
        place_ref, rows_ref = refs[:2]
    else:
        main_ref, edge_ref = refs[:2]
    (
        qkv_w,
        proj_w,
        fc1_w,
        fc2_w,
        vec_ref,
        qkv_b,
        fc1_b,
        bias_ref,
        heads_ref,
        wide_heads_ref,
        x_out,
        qkv_out,
        prob_out,
        att_out,
        mid_out,
        act_out,
        slope_out,
        y_out,
    ) = refs[2:20]
    step = pl.program_id(0)
    if layer == 0:
        spots = lax.broadcasted_iota(jnp.int32, (CHUNK, rows_ref.shape[0]), 1)
        pick = jnp.where(spots == place_ref[...], 1.0, 0.0).astype(bf16)
        x_out[...] = dot_nn(pick, rows_ref[...])
    else:
        whole_ref = refs[20]

        @pl.when(step == 0)
        def _():
            assemble_ahead(main_ref, edge_ref, whole_ref)

        x_out[...] = whole_ref[pl.ds(pl.multiple_of(step * CHUNK, CHUNK), CHUNK), :]
    x = x_out[...]
    normal, _ = norm_parts(x)
    hidden = (normal * vec_ref[4:5, :] + vec_ref[6:7, :]).astype(bf16)
    qkv_out[...] = (dot_nn(hidden, qkv_w[...]) + qkv_b[...]).astype(bf16)
    if layer == 1:
        apart = lax.broadcasted_iota(jnp.int32, (CELL, GROUP * CELL), 0) ^ lax.broadcasted_iota(
            jnp.int32, (CELL, GROUP * CELL), 1
        )
    for k in range(CHUNK_WINS):
        rows = slice(CELL * k, CELL * (k + 1))
        mixed = []
        for g in range(2):
            q = qkv_out[rows, 128 * g : 128 * g + 256]
            key = qkv_out[rows, D + 128 * g : D + 128 * g + 256]
            val = qkv_out[rows, 2 * D + 128 * g : 2 * D + 128 * g + 256]
            q_wide = jnp.concatenate([q] * GROUP, axis=0) * wide_heads_ref[g]
            lanes = slice(GROUP * CELL * g, GROUP * CELL * (g + 1))
            s = dot_nt(key, q_wide) * SCALE + bias_ref[:, lanes]
            if layer == 1:
                cut = mask_ref[step * CHUNK_WINS + k]
                s = jnp.where((apart & cut) == 0, s, MASKED)
            e = jnp.exp(s - jnp.max(s, axis=0, keepdims=True))
            prob = (e * (1.0 / jnp.sum(e, axis=0, keepdims=True))).astype(bf16)
            prob_out[rows, lanes] = prob
            spread = dot_tn(prob, val)
            mixed.append(gather_heads(spread, heads_ref, g))
        att_out[rows, :] = join_groups(*mixed).astype(bf16)
    mid = x + (dot_nn(att_out[...], proj_w[...]) + vec_ref[2:3, :])
    mid_out[...] = mid
    normal, _ = norm_parts(mid)
    hidden = (normal * vec_ref[5:6, :] + vec_ref[7:8, :]).astype(bf16)
    u = dot_nn(hidden, fc1_w[...]) + fc1_b[...]
    cdf = 0.5 * (1.0 + lax.erf(u * ROOT_HALF))
    act_out[...] = (u * cdf).astype(bf16)
    slope_out[...] = (cdf + u * (jnp.exp(-0.5 * u * u) * INV_ROOT_TAU)).astype(bf16)
    y = mid + (dot_nn(act_out[...], fc2_w[...]) + vec_ref[3:4, :])
    y_out[...] = y.astype(y_out.dtype)


def gather_heads(spread, heads_ref, g):
    total = None
    for h in range(GROUP):
        part = spread[CELL * h : CELL * (h + 1), :] * heads_ref[
            GROUP * g + h : GROUP * g + h + 1, 128 * g : 128 * g + 256
        ]
        total = part if total is None else total + part
    return total


def join_groups(low, high):
    return jnp.concatenate([low[:, :128], low[:, 128:] + high[:, :128], high[:, 128:]], axis=1)


def forward_layer(layer, masks, first, second, weights, bias, y_dtype):
    qkv_w, proj_w, fc1_w, fc2_w, vec, qkv_b, fc1_b = weights
    heads, wide = head_masks()
    tokens = 1024 if layer == 0 else first.shape[0]
    tokens = first.shape[0]
    ff = fc1_w.shape[1]
    if layer == 0:
        leading = [rows_of((CHUNK, 1)), whole(second.shape)]
        scratch = []
    else:
        leading = [whole(first.shape), whole(second.shape)]
        scratch = [pltpu.VMEM((tokens, D), f32)]
    operands = (
        qkv_w,
        proj_w,
        fc1_w,
        fc2_w,
        vec,
        qkv_b,
        fc1_b,
        bias,
        jnp.asarray(heads),
        jnp.asarray(wide, dtype=bf16),
    )
    outs = [
        ((tokens, D), f32),
        ((tokens, 3 * D), bf16),
        ((tokens, HEADS * CELL), bf16),
        ((tokens, D), bf16),
        ((tokens, D), f32),
        ((tokens, ff), bf16),
        ((tokens, ff), bf16),
        ((tokens, D), y_dtype),
    ]
    return pl.pallas_call(
        functools.partial(forward_kernel, layer),
        grid=(tokens // CHUNK,),
        in_specs=[pl.BlockSpec(memory_space=pltpu.SMEM)]
        + leading
        + [whole(operand.shape) for operand in operands],
        out_specs=[rows_of((CHUNK, shape[1])) for shape, _ in outs],
        out_shape=[jax.ShapeDtypeStruct(shape, dtype) for shape, dtype in outs],
        scratch_shapes=scratch,
        compiler_params=pltpu.CompilerParams(vmem_limit_bytes=VMEM_LIMIT),
        name=f"forward_{layer}",
    )(masks, first, second, *operands)


def backward_kernel(
    layer,
    main_ref,
    edge_ref,
    x_ref,
    qkv_ref,
    prob_ref,
    att_ref,
    mid_ref,
    act_ref,
    slope_ref,
    qkv_w,
    proj_w,
    fc1_w,
    fc2_w,
    vec_ref,
    heads_ref,
    wide_heads_ref,
    grad_out,
    qkv_g,
    proj_g,
    fc1_g,
    fc2_g,
    vec_g,
    fc1_bg,
    table_g,
    whole_ref,
    h1_ref,
    dt_ref,
    ga_ref,
    h2_ref,
    du_ref,
    gz_ref,
):
    step = pl.program_id(0)
    here = pl.ds(pl.multiple_of(step * CHUNK, CHUNK), CHUNK)

    @pl.when(step == 0)
    def _():
        if layer == 0:
            assemble_back(main_ref, edge_ref, whole_ref)
        else:
            assemble_ahead(main_ref, edge_ref, whole_ref)
        vec_g[...] = jnp.zeros_like(vec_g)
        fc1_bg[...] = jnp.zeros_like(fc1_bg)
        table_g[...] = jnp.zeros_like(table_g)

    upstream = whole_ref[here, :]
    low = upstream.astype(bf16)
    gz_ref[here, :] = low
    vec_g[3:4, :] += column_sum(low.astype(f32))
    du = (dot_nt(low, fc2_w[...]) * slope_ref[...].astype(f32)).astype(bf16)
    du_ref[here, :] = du
    fc1_bg[...] += column_sum(du.astype(f32))
    dn = dot_nt(du, fc1_w[...])
    normal, inverse = norm_parts(mid_ref[...])
    h2_ref[here, :] = (normal * vec_ref[5:6, :] + vec_ref[7:8, :]).astype(bf16)
    vec_g[5:6, :] += column_sum(dn * normal)
    vec_g[7:8, :] += column_sum(dn)
    mid_grad = upstream + norm_back(dn, normal, inverse, vec_ref[5:6, :])
    low = mid_grad.astype(bf16)
    ga_ref[here, :] = low
    vec_g[2:3, :] += column_sum(low.astype(f32))
    att_grad = dot_nt(low, proj_w[...]).astype(bf16)
    for k in range(CHUNK_WINS):
        rows = slice(CELL * k, CELL * (k + 1))
        there = pl.ds(pl.multiple_of(step * CHUNK + CELL * k, CELL), CELL)
        q_parts, k_parts, v_parts = [], [], []
        for g in range(2):
            q = qkv_ref[rows, 128 * g : 128 * g + 256]
            key = qkv_ref[rows, D + 128 * g : D + 128 * g + 256]
            val = qkv_ref[rows, 2 * D + 128 * g : 2 * D + 128 * g + 256]
            do = att_grad[rows, 128 * g : 128 * g + 256]
            q_wide = jnp.concatenate([q] * GROUP, axis=0) * wide_heads_ref[g]
            do_wide = jnp.concatenate([do] * GROUP, axis=0) * wide_heads_ref[g]
            lanes = slice(GROUP * CELL * g, GROUP * CELL * (g + 1))
            prob_low = prob_ref[rows, lanes]
            prob = prob_low.astype(f32)
            dp = dot_nt(val, do_wide)
            v_parts.append(dot_nn(prob_low, do_wide))
            weighted = prob * dp
            ds = (weighted - prob * column_sum(weighted)).astype(bf16)
            table_g[:, lanes] += ds.astype(f32)
            k_parts.append(dot_nn(ds, q_wide))
            q_parts.append(gather_heads(dot_tn(ds, key), heads_ref, g))
        dt_ref[there, 0:D] = (join_groups(*q_parts) * SCALE).astype(bf16)
        dt_ref[there, D : 2 * D] = (join_groups(*k_parts) * SCALE).astype(bf16)
        dt_ref[there, 2 * D : 3 * D] = join_groups(*v_parts).astype(bf16)
    dt = dt_ref[here, :]
    vec_g[0:1, :] += column_sum(dt[:, 0:D].astype(f32))
    vec_g[1:2, :] += column_sum(dt[:, 2 * D :].astype(f32))
    dn = dot_nt(dt, qkv_w[...])
    normal, inverse = norm_parts(x_ref[...])
    h1_ref[here, :] = (normal * vec_ref[4:5, :] + vec_ref[6:7, :]).astype(bf16)
    vec_g[4:5, :] += column_sum(dn * normal)
    vec_g[6:7, :] += column_sum(dn)
    grad_out[...] = (mid_grad + norm_back(dn, normal, inverse, vec_ref[4:5, :])).astype(
        grad_out.dtype
    )

    @pl.when(step == pl.num_programs(0) - 1)
    def _():
        fc2_g[...] = dot_tn(act_ref[...], gz_ref[...]).astype(bf16)
        fc1_g[...] = dot_tn(h2_ref[...], du_ref[...]).astype(bf16)
        proj_g[...] = dot_tn(att_ref[...], ga_ref[...]).astype(bf16)
        qkv_g[...] = dot_tn(h1_ref[...], dt_ref[...]).astype(bf16)


def backward_layer(layer, main, edge, saved, weights, grad_dtype):
    x, qkv, prob, att, mid, act, slope = saved
    qkv_w, proj_w, fc1_w, fc2_w, vec, _, _ = weights
    heads, wide = head_masks()
    tokens = main.shape[0]
    ff = fc1_w.shape[1]
    specs = [
        whole(main.shape),
        whole(edge.shape),
        rows_of((CHUNK, D)),
        rows_of((CHUNK, 3 * D)),
        rows_of((CHUNK, HEADS * CELL)),
        whole(att.shape),
        rows_of((CHUNK, D)),
        whole(act.shape),
        rows_of((CHUNK, ff)),
    ]
    operands = (
        qkv_w,
        proj_w,
        fc1_w,
        fc2_w,
        vec,
        jnp.asarray(heads),
        jnp.asarray(wide, dtype=bf16),
    )
    outs = [
        ((tokens, D), grad_dtype, rows_of((CHUNK, D))),
        (qkv_w.shape, bf16, whole(qkv_w.shape)),
        (proj_w.shape, bf16, whole(proj_w.shape)),
        (fc1_w.shape, bf16, whole(fc1_w.shape)),
        (fc2_w.shape, bf16, whole(fc2_w.shape)),
        (vec.shape, f32, whole(vec.shape)),
        ((1, ff), f32, whole((1, ff))),
        ((CELL, HEADS * CELL), f32, whole((CELL, HEADS * CELL))),
    ]
    return pl.pallas_call(
        functools.partial(backward_kernel, layer),
        grid=(tokens // CHUNK,),
        in_specs=specs + [whole(operand.shape) for operand in operands],
        out_specs=[spec for _, _, spec in outs],
        out_shape=[jax.ShapeDtypeStruct(shape, dtype) for shape, dtype, _ in outs],
        scratch_shapes=[
            pltpu.VMEM((tokens, D), f32),
            pltpu.VMEM((tokens, D), bf16),
            pltpu.VMEM((tokens, 3 * D), bf16),
            pltpu.VMEM((tokens, D), bf16),
            pltpu.VMEM((tokens, D), bf16),
            pltpu.VMEM((tokens, ff), bf16),
            pltpu.VMEM((tokens, D), bf16),
        ],
        compiler_params=pltpu.CompilerParams(vmem_limit_bytes=VMEM_LIMIT),
        name=f"backward_{layer}",
    )(main, edge, x, qkv, prob, att, mid, act, slope, *operands)


def shifted_rows(value, steps):
    count = lax.axis_size("row")
    pairs = [(source, (source + steps) % count) for source in range(count)]
    return lax.ppermute(value, "row", pairs)


def edge_rows(values, first_window, first_sub):
    shaped = values.reshape(-1, CELL, values.shape[-1])
    part = shaped[first_window : first_window + WIN_COLS, first_sub * BLOCK : (first_sub + 2) * BLOCK]
    return part.reshape(-1, values.shape[-1]).astype(bf16)


def exchange(values):
    return lax.all_to_all(values, ("clip", "row"), split_axis=0, concat_axis=0, tiled=True)


def body(
    inputs,
    cotangent,
    source_of,
    split_row,
    qkv_weight,
    qv_bias,
    proj_weight,
    proj_bias,
    fc1_weight,
    fc1_bias,
    fc2_weight,
    fc2_bias,
    norm_gain,
    norm_bias,
    rel_table,
):
    clip_count = lax.axis_size("clip")
    row_count = lax.axis_size("row")
    tokens = inputs.shape[0]
    block_rows = tokens // (clip_count * row_count)
    grid_rows = tokens // GRID_COLS
    slot_rows = grid_rows * row_count
    window_rows = grid_rows // WIN
    part = D // row_count

    placing = source_of // tokens * block_rows + source_of % block_rows
    placing = placing.reshape(window_rows, 2, SHIFT, WIN_COLS, 2, SHIFT)
    placing = placing.transpose(0, 3, 1, 4, 2, 5).reshape(tokens)
    arrived = exchange(inputs)
    incoming = exchange(cotangent)

    middle = lax.axis_index("row") * grid_rows + WIN * (1 + jnp.arange(window_rows))
    row_cut = ((middle == split_row[0]) | (middle == slot_rows)).astype(jnp.int32)
    col_cut = (jnp.arange(WIN_COLS) == WIN_COLS - 1).astype(jnp.int32)
    cuts = (32 * row_cut[:, None] + 16 * col_cut[None, :]).reshape(-1)

    vectors = jnp.concatenate(
        [
            qv_bias,
            proj_bias[:, None],
            fc2_bias[:, None],
            norm_gain,
            norm_bias,
            fc1_bias.reshape(2, -1, part),
        ],
        axis=1,
    )
    vectors = lax.all_gather(vectors, "row", axis=0)
    ff = fc1_weight.shape[2]
    fc1_row = vectors[:, :, 8:].transpose(1, 0, 2, 3).reshape(2, 1, ff).astype(f32)
    vec_rows = vectors[:, :, :8].transpose(1, 2, 0, 3).reshape(2, 8, D).astype(f32)
    qkv_row = jnp.concatenate(
        [vec_rows[:, 0:1], jnp.zeros((2, 1, D), f32), vec_rows[:, 1:2]], axis=2
    )
    weights = []
    for layer in range(2):
        gathered = [
            lax.all_gather(weight[layer], "row", axis=0, tiled=True)
            for weight in (qkv_weight, proj_weight, fc1_weight, fc2_weight)
        ]
        weights.append((*gathered, vec_rows[layer], qkv_row[layer], fc1_row[layer]))
    bias = bias_tables(rel_table)

    *saved_one, layer_one = forward_layer(
        0, cuts, placing.reshape(tokens, 1), arrived, weights[0], bias[0], f32
    )
    incoming = place_rows(placing.reshape(tokens, 1), incoming)
    ahead = shifted_rows(edge_rows(layer_one, 0, 0), -1)
    ahead_grad = shifted_rows(edge_rows(incoming, 0, 0), -1)
    *saved_two, layer_two = forward_layer(1, cuts, layer_one, ahead, weights[1], bias[1], bf16)
    last = (window_rows - 1) * WIN_COLS
    behind = shifted_rows(edge_rows(layer_two, last, 2), 1)
    out_rows = unplace_rows(placing.reshape(1, tokens), layer_two, behind)
    output = exchange(out_rows)
    grad_two, *grads_two = backward_layer(1, incoming, ahead_grad, saved_two, weights[1], f32)
    behind_grad = shifted_rows(edge_rows(grad_two, last, 2), 1)
    grad_one, *grads_one = backward_layer(0, grad_two, behind_grad, saved_one, weights[0], bf16)
    grad_rows = unplace_plain(placing.reshape(1, tokens), grad_one)
    input_grad = exchange(grad_rows).astype(f32)

    totals = []
    for one, two in zip(grads_one[:4], grads_two[:4]):
        pair = []
        for value in (one, two):
            value = lax.psum_scatter(value, "row", scatter_dimension=0, tiled=True)
            pair.append(lax.psum(value, "clip").astype(f32))
        totals.append(jnp.stack(pair))
    table = table_sums(grads_one[6], grads_two[6])
    small = jnp.concatenate(
        [
            jnp.stack([grads_one[4], grads_two[4]]).reshape(2, -1),
            jnp.stack([grads_one[5], grads_two[5]]).reshape(2, -1),
            table.reshape(2, -1),
        ],
        axis=1,
    )
    small = lax.psum(small, ("clip", "row"))
    at = lax.axis_index("row")
    vec_total = small[:, : 8 * D].reshape(2, 8, D)
    vec_total = lax.dynamic_slice_in_dim(vec_total, at * part, part, axis=2)
    fc1_total = lax.dynamic_slice_in_dim(
        small[:, 8 * D : 8 * D + ff], at * (ff // row_count), ff // row_count, axis=1
    )
    table_total = small[:, 8 * D + ff :].reshape(2, HEADS, TABLE_PAD)[:, :, :TABLE]
    return (
        output,
        input_grad,
        totals[0],
        vec_total[:, 0:2],
        totals[1],
        vec_total[:, 2],
        totals[2],
        fc1_total,
        totals[3],
        vec_total[:, 3],
        vec_total[:, 4:6],
        vec_total[:, 6:8],
        table_total.transpose(0, 2, 1),
    )


def unplace_plain_kernel(place_ref, rows_ref, out_ref):
    tokens = rows_ref.shape[0]
    spots = lax.broadcasted_iota(jnp.int32, (CHUNK, tokens), 0) + pl.program_id(0) * CHUNK
    pick = jnp.where(spots == place_ref[...], 1.0, 0.0).astype(bf16)
    out_ref[...] = dot_nn(pick, rows_ref[...]).astype(out_ref.dtype)


def unplace_plain(place, rows):
    tokens, width = rows.shape
    return pl.pallas_call(
        unplace_plain_kernel,
        grid=(tokens // CHUNK,),
        in_specs=[whole((1, tokens)), whole((tokens, width))],
        out_specs=rows_of((CHUNK, width)),
        out_shape=jax.ShapeDtypeStruct((tokens, width), bf16),
        name="unplace_plain",
    )(place, rows)


def solution(mesh):
    placed = (
        P(("clip", "row"), None),
        P(("clip", "row"), None),
        P(("clip", "row")),
        P("clip"),
        P(None, "row", None),
        P(None, None, "row"),
        P(None, "row", None),
        P(None, "row"),
        P(None, "row", None),
        P(None, "row"),
        P(None, "row", None),
        P(None, "row"),
        P(None, None, "row"),
        P(None, None, "row"),
        P(),
    )
    return jax.shard_map(
        body,
        mesh=mesh,
        in_specs=placed,
        out_specs=(
            P(("clip", "row"), None),
            P(("clip", "row"), None),
            P(None, "row", None),
            P(None, None, "row"),
            P(None, "row", None),
            P(None, "row"),
            P(None, "row", None),
            P(None, "row"),
            P(None, "row", None),
            P(None, "row"),
            P(None, None, "row"),
            P(None, None, "row"),
            P(),
        ),
        check_vma=False,
    )
```

time: 909 us -> 670 us (0.74)
  local copies, waits for them, and re-layouts: 261 us -> 22.7 us
  waiting for transfers between devices: 224 us -> 388 us
  matrix products: 155 us -> 0 us
  Pallas kernels: 0 us -> 128 us
  other arithmetic: 90.8 us -> 11.1 us
  blocking collectives: 129 us -> 70.6 us
    dot_general x44 -> x0, matrix products: 155 us -> none  [the longest x2 34.5 us: layer_forward(): jnp.dot(hidden_two, w_up, preferred_element_type=jnp.float32)]
    psum x1 -> x2, waiting for transfers between devices: 42.4 us -> 187 us  [the longest x1 124 us: body(): small = lax.psum(small, ('clip', 'row'))]
    pallas_call x0 -> x9, Pallas kernels: none -> 128 us  [the longest x2 59.6 us: backward_layer(): pl.pallas_call(functools.partial(backward_kernel, layer), grid=(tokens //...]
    reduce_scatter x4 -> x8, waiting for transfers between devices: 51.6 us -> 169 us  [body(): value = lax.psum_scatter(value, 'row', scatter_dimension=0, tiled=True)]
    unnamed x20 -> x14, waiting for transfers between devices: 113 us -> 4.85 us
    another operation x41 -> x2, local copies, waits for them, and re-layouts: 103 us -> 1.75 us  [the longest x1 0.99 us: body(): placing.reshape(tokens, 1)]
    psum x2 -> x0, blocking collectives: 56.8 us -> none  [the longest x1 40 us: body(): table_total = lax.psum(stacked[10], ('clip', 'row'))]
    concatenate x7 -> x2, local copies, waits for them, and re-layouts: 41.5 us -> 0.06 us  [the longest x1 0.05 us: body(): jnp.concatenate([qv_bias, proj_bias[:, None], fc2_bias[:, None], norm_gai...]
  transfers between devices with their start and end apart: 21 -> 22, of which waited for: 12 -> 12; matrix products, arithmetic and copies ran while one was open for 30% -> 3% of each run, Pallas kernels for 0% -> 15%
where the time goes in v1:
time: 670 us; the launch traced here: 661 us
  waiting for transfers between devices  388 us (58%)
  Pallas kernels  128 us (19%)
  blocking collectives  70.6 us (11%)
  starting transfers between devices  25.3 us (4%)
  local copies, waits for them, and re-layouts  22.7 us (3%)
  between operations  15.5 us (2%)
  other arithmetic  11.1 us (2%)
    reduce_scatter x8, waiting for transfers between devices, body(): value = lax.psum_scatter(value, 'row', scatter_dimension=0, tiled=True)  169 us
    psum x1, waiting for transfers between devices, body(): small = lax.psum(small, ('clip', 'row'))  124 us
    psum x1, waiting for transfers between devices, body(): pair.append(lax.psum(value, 'clip').astype(f32))  62.9 us
    all_gather x4, blocking collectives, body(): lax.all_gather(weight[layer], 'row', axis=0, tiled=True)  60.4 us
    pallas_call x2, Pallas kernels, backward_layer(): pl.pallas_call(functools.partial(backward_kernel, layer), grid=(tokens //...  59.6 us
    pallas_call x2, Pallas kernels, forward_layer(): pl.pallas_call(functools.partial(forward_kernel, layer), grid=(tokens //...  41.2 us
    all_to_all x4, starting transfers between devices, exchange(): lax.all_to_all(values, ('clip', 'row'), split_axis=0, concat_axis=0, tile...  20.5 us
    ppermute x4, waiting for transfers between devices, shifted_rows(): return lax.ppermute(value, 'row', pairs)  14.7 us
  transfers between devices with their start and end apart: 22, of which 12 were waited for; matrix products, arithmetic and copies ran while one was open for 3% of the time, Pallas kernels for 15%

profile of v1, /device:TPU:0, one launch (start us, length us, event | category | flops | bytes accessed | tf_op | source)
XLA Modules:
  0.0 660.9 jit_solution(6320731584376766693)
XLA Ops:
  7.2 2.0 fusion.6
  9.3 0.9 fusion.5
  11.0 7.3 %all-to-all-start.2 = ((bf16[32,32,384]{2,1,0:T(8,128)(2,1)}), bf16[32,32,384]{2,1,0:T(8,128)(2,1)S(1)}, u32[]{:S(2)}, u32[]{:S(2)}) async-start(bf16[32,32,384]{2,1,0:T(8,128)(2,1)} %bitcast.28), calls=%async_computation.2 | async-start | bytes 1572864 | tf_op jit(solution)/shard_map/all_to_all | solution.py:573
  19.7 10.3 %all-gather.4 = bf16[8,12,96]{2,1,0:T(8,128)(2,1)S(1)} all-gather(bf16[2,12,96]{2,1,0:T(8,128)(2,1)S(1)} %concatenate.10), channel_id=6, replica_groups=mesh['clip'=8,'row'=4] {'row'}, dimensions={0}, use_global_device_ids=true | all-gather | bytes 23040 | tf_op jit(solution)/shard_map/all_gather | solution.py:624
  30.4 11.5 %all-gather.1 = bf16[1,384,384]{2,1,0:T(8,128)(2,1)} all-gather(bf16[1,96,384]{2,1,0:T(8,128)(2,1)S(1)} %get-tuple-element.96), channel_id=3, replica_groups=mesh['clip'=8,'row'=4] {'row'}, dimensions={1}, use_global_device_ids=true | all-gather | bytes 368640 | tf_op jit(solution)/shard_map/all_gather | solution.py:634
  42.8 1.0 reshape_reshape.10.refs_0_.place_ref
  47.2 6.4 bias_tables.1
  53.7 6.6 %all-to-all-start = ((bf16[32,32,384]{2,1,0:T(8,128)(2,1)}), bf16[32,32,384]{2,1,0:T(8,128)(2,1)S(1)}, u32[]{:S(2)}, u32[]{:S(2)}) async-start(bf16[32,32,384]{2,1,0:T(8,128)(2,1)} %bitcast.2), calls=%async_computation | async-start | bytes 1572864 | tf_op jit(solution)/shard_map/all_to_all | solution.py:573
  60.4 25.1 %all-gather = bf16[1,384,1152]{2,1,0:T(8,128)(2,1)} all-gather(bf16[1,96,1152]{2,1,0:T(8,128)(2,1)S(1)} %get-tuple-element.94), channel_id=2, replica_groups=mesh['clip'=8,'row'=4] {'row'}, dimensions={1}, use_global_device_ids=true | all-gather | bytes 1105920 | tf_op jit(solution)/shard_map/all_gather | solution.py:634
  85.5 0.8 slice_bitcast_fusion
  86.9 4.6 place_rows.1.main_ref
  91.5 0.9 slice.152
  92.4 1.2 collective-permute-start.2
  93.7 0.9 copy-done
  94.5 21.2 %forward_0.1 = (f32[1024,384]{1,0:T(8,128)}, bf16[1024,1152]{1,0:T(8,128)(2,1)}, bf16[1024,1024]{1,0:T(8,128)(2,1)}, bf16[1024,384]{1,0:T(8,128)(2,1)}, f32[1024...) custom-call(s32[16]{0:T(128)} %add.94.mask_ref, ...), custom_call_target="tpu_custom_call" | custom-call | tf_op jit(solution)/shard_map/forward_0/pallas_call | solution.py:382
  115.7 1.5 convert.23
  117.2 1.6 collective-permute-start
  118.9 10.0 %all-gather.6 = bf16[1,384,384]{2,1,0:T(8,128)(2,1)} all-gather(bf16[1,96,384]{2,1,0:T(8,128)(2,1)S(1)} %get-tuple-element.95), channel_id=8, replica_groups=mesh['clip'=8,'row'=4] {'row'}, dimensions={1}, use_global_device_ids=true | all-gather | bytes 368640 | tf_op jit(solution)/shard_map/all_gather | solution.py:634
  128.9 13.8 %all-gather.5 = bf16[1,384,1152]{2,1,0:T(8,128)(2,1)} all-gather(bf16[1,96,1152]{2,1,0:T(8,128)(2,1)S(1)} %get-tuple-element.93), channel_id=7, replica_groups=mesh['clip'=8,'row'=4] {'row'}, dimensions={1}, use_global_device_ids=true | all-gather | bytes 1105920 | tf_op jit(solution)/shard_map/all_gather | solution.py:634
  142.7 5.0 all-gather.20.cloned.1.call-done
  148.4 20.0 %forward_1.1 = (f32[1024,384]{1,0:T(8,128)}, bf16[1024,1152]{1,0:T(8,128)(2,1)}, bf16[1024,1024]{1,0:T(8,128)(2,1)}, bf16[1024,384]{1,0:T(8,128)(2,1)}, f32[1024...) custom-call(s32[16]{0:T(128)} %add.94.mask_ref, ...), custom_call_target="tpu_custom_call" | custom-call | tf_op jit(solution)/shard_map/forward_1/pallas_call | solution.py:382
  169.1 29.8 %backward_1.1 = (f32[1024,384]{1,0:T(8,128)}, bf16[384,1152]{1,0:T(8,128)(2,1)}, bf16[384,384]{1,0:T(8,128)(2,1)}, bf16[384,1536]{1,0:T(8,128)(2,1)}, bf16[1536,...) custom-call(bf16[1024,384]{1,0:T(8,128)(2,1)} %place_rows.1.main_ref, ...), custom_call_target="tpu_custom_call" | custom-call | tf_op jit(solution)/shard_map/backward_1/pallas_call | solution.py:540
  199.0 1.5 convert.24
  200.5 0.9 collective-permute-start.3
  201.4 7.2 %collective-permute-done.3.edge_ref = bf16[256,384]{1,0:T(8,128)(2,1)S(1)} collective-permute-done((bf16[256,384]{1,0:T(8,128)(2,1)S(1)}, bf16[256,384]{1,0:T(8,128)(2,1)S(1)}, u32[]{:S(2)}, u32[]{:S(2)}) %collective-permute-start.3) | collective-permute-done | bytes 196640 | tf_op jit(solution)/shard_map/ppermute | solution.py:563
  209.3 29.8 %backward_0.1 = (bf16[1024,384]{1,0:T(8,128)(2,1)}, bf16[384,1152]{1,0:T(8,128)(2,1)}, bf16[384,384]{1,0:T(8,128)(2,1)}, bf16[384,1536]{1,0:T(8,128)(2,1)}, bf16...) custom-call(f32[1024,384]{1,0:T(8,128)} %get-tuple-element.54.main_ref, ...), custom_call_target="tpu_custom_call" | custom-call | tf_op jit(solution)/shard_map/backward_0/pallas_call | solution.py:540
  242.7 1.0 slice.151
  244.5 7.5 %collective-permute-done.1.edge_ref = bf16[256,384]{1,0:T(8,128)(2,1)S(1)} collective-permute-done((bf16[256,384]{1,0:T(8,128)(2,1)S(1)}, bf16[256,384]{1,0:T(8,128)(2,1)S(1)}, u32[]{:S(2)}, u32[]{:S(2)}) %collective-permute-start.1) | collective-permute-done | bytes 196640 | tf_op jit(solution)/shard_map/ppermute | solution.py:563
  252.7 3.9 unplace_rows.1
  256.6 3.8 all-to-all-start.1
  261.0 3.8 unplace_plain.1
  264.8 8.5 %table_sums.1 = f32[2,16,256]{2,1,0:T(8,128)} custom-call(f32[64,1024]{1,0:T(8,128)} %get-tuple-element.69.one_ref, f32[64,1024]{1,0:T(8,128)} %get-tuple-element.70.two_ref, f32[2,256,128]{2,1,0:T(8,128)} %constant.68.clone.lanes_ref, f32[64,64]{1,0:T(8,128)} %constant.72.clone.back_ref), custom_call_target="tpu_custom_call" | custom-call | tf_op jit(solution)/shard_map/table_sums/pallas_call | solution.py:163
  274.2 7.5 %all-to-all-done.1 = bf16[32,32,384]{2,1,0:T(8,128)(2,1)S(1)} async-done(((bf16[32,32,384]{2,1,0:T(8,128)(2,1)}), bf16[32,32,384]{2,1,0:T(8,128)(2,1)S(1)}, u32[]{:S(2)}, u32[]{:S(2)}) %all-to-all-start.1) | async-done | bytes 786464 | tf_op jit(solution)/shard_map/all_to_all | solution.py:573
  281.8 2.9 all-to-all-start.3
  285.5 12.3 %reduce-scatter.11.cloned.1.call-done = bf16[96,1152]{1,0:T(8,128)(2,1)} async-done(((bf16[384,1152]{1,0:T(8,128)(2,1)}), bf16[96,1152]{1,0:T(8,128)(2,1)}) %reduce-scatter.11.cloned.1.call-update) | async-done | bytes 221200 | tf_op jit(solution)/shard_map/reduce_scatter | solution.py:661
  297.8 29.5 %reduce-scatter.9.cloned.1.call-done = bf16[96,1152]{1,0:T(8,128)(2,1)} async-done(((bf16[384,1152]{1,0:T(8,128)(2,1)}), bf16[96,1152]{1,0:T(8,128)(2,1)}) %reduce-scatter.9.cloned.1.call-update) | async-done | bytes 221200 | tf_op jit(solution)/shard_map/reduce_scatter | solution.py:661
  327.2 32.1 %reduce-scatter.19.cloned.1.call-done = bf16[96,1536]{1,0:T(8,128)(2,1)} async-done(((bf16[384,1536]{1,0:T(8,128)(2,1)}), bf16[96,1536]{1,0:T(8,128)(2,1)}) %reduce-scatter.19.cloned.1.call-update) | async-done | bytes 294928 | tf_op jit(solution)/shard_map/reduce_scatter | solution.py:661
  359.3 31.9 %reduce-scatter.23.cloned.1.call-done = bf16[384,384]{1,0:T(8,128)(2,1)} async-done(((bf16[1536,384]{1,0:T(8,128)(2,1)}), bf16[384,384]{1,0:T(8,128)(2,1)}) %reduce-scatter.23.cloned.1.call-update) | async-done | bytes 294928 | tf_op jit(solution)/shard_map/reduce_scatter | solution.py:661
  391.2 31.5 %reduce-scatter.17.cloned.1.call-done = bf16[96,1536]{1,0:T(8,128)(2,1)} async-done(((bf16[384,1536]{1,0:T(8,128)(2,1)}), bf16[96,1536]{1,0:T(8,128)(2,1)}) %reduce-scatter.17.cloned.1.call-update) | async-done | bytes 294928 | tf_op jit(solution)/shard_map/reduce_scatter | solution.py:661
  422.7 31.3 %reduce-scatter.21.cloned.1.call-done = bf16[384,384]{1,0:T(8,128)(2,1)} async-done(((bf16[1536,384]{1,0:T(8,128)(2,1)}), bf16[384,384]{1,0:T(8,128)(2,1)}) %reduce-scatter.21.cloned.1.call-update) | async-done | bytes 294928 | tf_op jit(solution)/shard_map/reduce_scatter | solution.py:661
  454.1 124.0 %all-reduce.5.cloned.1.call-done = f32[2,8704]{1,0:T(2,128)} async-done(((f32[2,8704]{1,0:T(2,128)}), f32[2,8704]{1,0:T(2,128)}) %all-reduce.5.cloned.1.call-update) | async-done | bytes 69648 | tf_op jit(solution)/shard_map/psum | solution.py:673
  582.8 1.3 bitcast_convert_fusion
  584.2 62.9 %all-reduce.7.cloned.1.call-done = (bf16[1,96,1152]{2,1,0:T(8,128)(2,1)}, bf16[1,96,1152]{2,1,0:T(8,128)(2,1)}, bf16[1,96,384]{2,1,0:T(8,128)(2,1)}, bf16[1,96,3...) async-done(((bf16[1,96,1152]{2,1,0:T(8,128)(2,1)}, ...) | async-done | bytes 1769488 | tf_op jit(solution)/shard_map/psum | solution.py:662
  647.0 2.1 maximum_convert_fusion.2
  649.2 1.7 maximum_convert_fusion.3
  650.8 1.1 maximum_convert_fusion
  651.9 1.1 maximum_convert_fusion.1
  653.0 0.9 copy.103
  (139 shorter events, 21.1 us)
Async XLA Ops:
  7.2 2.2 copy-start.3
  7.2 86.5 %all-gather.14.cloned.1.call-start = ((), (), s32[]{:S(2)}) async-start(), calls=%async_computation.21 | async-start | bytes 1474560 | tf_op jit(solution)/shard_map/all_gather | solution.py:634
  9.2 10.3 %copy-start.24 = (bf16[2,96]{1,0:T(2,128)(2,1)S(1)}, bf16[2,96]{1,0:T(2,128)(2,1)}, u32[]{:S(2)}) copy-start(bf16[2,96]{1,0:T(2,128)(2,1)} %param.34) | copy-start | bytes 1156
  9.2 10.3 %copy-start.25 = (bf16[2,96]{1,0:T(2,128)(2,1)S(1)}, bf16[2,96]{1,0:T(2,128)(2,1)}, u32[]{:S(2)}) copy-start(bf16[2,96]{1,0:T(2,128)(2,1)} %param.38) | copy-start | bytes 1156
  9.2 10.3 %copy-start.20 = (bf16[2,384]{1,0:T(2,128)(2,1)S(1)}, bf16[2,384]{1,0:T(2,128)(2,1)}, u32[]{:S(2)}) copy-start(bf16[2,384]{1,0:T(2,128)(2,1)} %param.36) | copy-start | bytes 4612
  9.2 10.4 %copy-start.21 = (bf16[2,2,96]{2,1,0:T(2,128)(2,1)S(1)}, bf16[2,2,96]{2,1,0:T(2,128)(2,1)}, u32[]{:S(2)}) copy-start(bf16[2,2,96]{2,1,0:T(2,128)(2,1)} %param.32) | copy-start | bytes 2308
  9.3 10.4 %copy-start.22 = (bf16[2,2,96]{2,1,0:T(2,128)(2,1)S(1)}, bf16[2,2,96]{2,1,0:T(2,128)(2,1)}, u32[]{:S(2)}) copy-start(bf16[2,2,96]{2,1,0:T(2,128)(2,1)} %param.39) | copy-start | bytes 2308
  9.3 10.4 %copy-start.23 = (bf16[2,2,96]{2,1,0:T(2,128)(2,1)S(1)}, bf16[2,2,96]{2,1,0:T(2,128)(2,1)}, u32[]{:S(2)}) copy-start(bf16[2,2,96]{2,1,0:T(2,128)(2,1)} %param.40) | copy-start | bytes 2308
  9.3 84.4 %all-gather.16.cloned.1.call-start = ((), (), s32[]{:S(2)}) async-start(), calls=%async_computation.22 | async-start | bytes 1474560 | tf_op jit(solution)/shard_map/all_gather | solution.py:634
  10.2 20.0 %copy-start.19 = (s32[1024]{0:T(1024)S(1)}, s32[1024]{0:T(1024)}, u32[]{:S(2)}) copy-start(s32[1024]{0:T(1024)} %param.29) | copy-start | bytes 12292
  10.2 20.1 %copy-start.13 = (bf16[2,96,384]{2,1,0:T(8,128)(2,1)S(1)}, bf16[2,96,384]{2,1,0:T(8,128)(2,1)}, u32[]{:S(2)}) copy-start(bf16[2,96,384]{2,1,0:T(8,128)(2,1)} %param.33) | copy-start | bytes 442372
  10.2 20.1 %copy-start.4 = (bf16[2,96,1152]{2,1,0:T(8,128)(2,1)S(1)}, bf16[2,96,1152]{2,1,0:T(8,128)(2,1)}, u32[]{:S(2)}) copy-start(bf16[2,96,1152]{2,1,0:T(8,128)(2,1)} %param.31) | copy-start | bytes 1327108
  10.2 132.4 %all-gather.18.cloned.1.call-start = ((), (), s32[]{:S(2)}) async-start(), calls=%async_computation.23 | async-start | bytes 1474560 | tf_op jit(solution)/shard_map/all_gather | solution.py:634
  11.0 42.7 %all-to-all-start.2 = ((bf16[32,32,384]{2,1,0:T(8,128)(2,1)}), bf16[32,32,384]{2,1,0:T(8,128)(2,1)S(1)}, u32[]{:S(2)}, u32[]{:S(2)}) async-start(bf16[32,32,384]{2,1,0:T(8,128)(2,1)} %bitcast.28), calls=%async_computation.2 | async-start | bytes 1572864 | tf_op jit(solution)/shard_map/all_to_all | solution.py:573
  18.3 129.4 %all-gather.20.cloned.1.call-start = ((), (), s32[]{:S(2)}) async-start(), calls=%async_computation.24 | async-start | bytes 1474560 | tf_op jit(solution)/shard_map/all_gather | solution.py:634
  19.7 26.9 %copy-start.14 = (f32[2,225,16]{1,2,0:T(8,128)S(1)}, f32[2,225,16]{1,2,0:T(8,128)}, u32[]{:S(2)}) copy-start(f32[2,225,16]{1,2,0:T(8,128)} %param.41) | copy-start | bytes 86404
  53.7 31.8 %copy-start.2 = (f32[2,64,1024]{2,1,0:T(8,128)S(1)}, f32[2,64,1024]{2,1,0:T(8,128)}, u32[]{:S(2)}) copy-start(f32[2,64,1024]{2,1,0:T(8,128)} %bias_tables.1) | copy-start | bytes 1572868
  53.7 32.6 %copy-start.1 = (bf16[32,32,384]{2,1,0:T(8,128)(2,1)}, bf16[32,32,384]{2,1,0:T(8,128)(2,1)S(1)}, u32[]{:S(2)}) copy-start(bf16[32,32,384]{2,1,0:T(8,128)(2,1)S(1)} %all-to-all-done.2) | copy-start | bytes 2359300
  53.7 40.0 %all-to-all-start = ((bf16[32,32,384]{2,1,0:T(8,128)(2,1)}), bf16[32,32,384]{2,1,0:T(8,128)(2,1)S(1)}, u32[]{:S(2)}, u32[]{:S(2)}) async-start(bf16[32,32,384]{2,1,0:T(8,128)(2,1)} %bitcast.2), calls=%async_computation | async-start | bytes 1572864 | tf_op jit(solution)/shard_map/all_to_all | solution.py:573
  60.3 225.1 %reduce-scatter.15.cloned.1.call-start = ((), (), s32[]{:S(2)}) async-start(), calls=%async_computation.16 | async-start | bytes 368640 | tf_op jit(solution)/shard_map/reduce_scatter | solution.py:661
  92.4 76.0 %collective-permute-start.2 = (bf16[256,384]{1,0:T(8,128)(2,1)S(1)}, bf16[256,384]{1,0:T(8,128)(2,1)S(1)}, u32[]{:S(2)}, u32[]{:S(2)}) collective-permute-start(bf16[256,384]{1,0:T(8,128)(2,1)S(1)} %bitcast.109), channel_id=1, source_target_pairs={{0,3},{1,0},{2,1},{3,2},{4,7},{5,4},{6,5},{7,6},{8,11},{9,8},{10,9... | collective-permute-start | bytes 589832 | tf_op jit(solution)/shard_map/ppermute | solution.py:563
  93.6 0.9 copy-start
  117.2 30.5 %collective-permute-start = (bf16[256,384]{1,0:T(8,128)(2,1)S(1)}, bf16[256,384]{1,0:T(8,128)(2,1)S(1)}, u32[]{:S(2)}, u32[]{:S(2)}) collective-permute-start(bf16[256,384]{1,0:T(8,128)(2,1)S(1)} %bitcast.110), channel_id=1, source_target_pairs={{0,3},{1,0},{2,1},{3,2},{4,7},{5,4},{6,5},{7,6},{8,11},{9,8},{10,9... | collective-permute-start | bytes 589832 | tf_op jit(solution)/shard_map/ppermute | solution.py:563
  147.7 0.7 copy-start.11
  168.4 0.7 copy-start.9
  198.9 86.5 %reduce-scatter.13.cloned.1.call-start = ((), (), s32[]{:S(2)}) async-start(), calls=%async_computation.15 | async-start | bytes 368640 | tf_op jit(solution)/shard_map/reduce_scatter | solution.py:661
  200.5 8.1 %collective-permute-start.3 = (bf16[256,384]{1,0:T(8,128)(2,1)S(1)}, bf16[256,384]{1,0:T(8,128)(2,1)S(1)}, u32[]{:S(2)}, u32[]{:S(2)}) collective-permute-start(bf16[256,384]{1,0:T(8,128)(2,1)S(1)} %bitcast.112), channel_id=1, source_target_pairs={{0,1},{1,2},{2,3},{3,0},{4,5},{5,6},{6,7},{7,4},{8,9},{9,10},{10,1... | collective-permute-start | bytes 589832 | tf_op jit(solution)/shard_map/ppermute | solution.py:563
  208.6 0.7 copy-start.10
  239.1 58.7 %reduce-scatter.11.cloned.1.call-start = ((), (), s32[]{:S(2)}) async-start(), calls=%async_computation.13 | async-start | bytes 1105920 | tf_op jit(solution)/shard_map/reduce_scatter | solution.py:661
  239.9 87.4 %reduce-scatter.9.cloned.1.call-start = ((), (), s32[]{:S(2)}) async-start(), calls=%async_computation.12 | async-start | bytes 1105920 | tf_op jit(solution)/shard_map/reduce_scatter | solution.py:661
  240.6 118.7 %reduce-scatter.19.cloned.1.call-start = ((), (), s32[]{:S(2)}) async-start(), calls=%async_computation.18 | async-start | bytes 1474560 | tf_op jit(solution)/shard_map/reduce_scatter | solution.py:661
  241.3 149.9 %reduce-scatter.23.cloned.1.call-start = ((), (), s32[]{:S(2)}) async-start(), calls=%async_computation.20 | async-start | bytes 1474560 | tf_op jit(solution)/shard_map/reduce_scatter | solution.py:661
  241.9 180.8 %reduce-scatter.17.cloned.1.call-start = ((), (), s32[]{:S(2)}) async-start(), calls=%async_computation.17 | async-start | bytes 1474560 | tf_op jit(solution)/shard_map/reduce_scatter | solution.py:661
  243.6 8.4 %collective-permute-start.1 = (bf16[256,384]{1,0:T(8,128)(2,1)S(1)}, bf16[256,384]{1,0:T(8,128)(2,1)S(1)}, u32[]{:S(2)}, u32[]{:S(2)}) collective-permute-start(bf16[256,384]{1,0:T(8,128)(2,1)S(1)} %bitcast.111), channel_id=1, source_target_pairs={{0,1},{1,2},{2,3},{3,0},{4,5},{5,6},{6,7},{7,4},{8,9},{9,10},{10,1... | collective-permute-start | bytes 589832 | tf_op jit(solution)/shard_map/ppermute | solution.py:563
  252.0 0.7 copy-start.12
  256.6 4.4 copy-start.15
  256.6 25.1 %all-to-all-start.1 = ((bf16[32,32,384]{2,1,0:T(8,128)(2,1)}), bf16[32,32,384]{2,1,0:T(8,128)(2,1)S(1)}, u32[]{:S(2)}, u32[]{:S(2)}) async-start(bf16[32,32,384]{2,1,0:T(8,128)(2,1)} %bitcast.91), calls=%async_computation.1 | async-start | bytes 1572864 | tf_op jit(solution)/shard_map/all_to_all | solution.py:573
  260.4 193.7 %reduce-scatter.21.cloned.1.call-start = ((), (), s32[]{:S(2)}) async-start(), calls=%async_computation.19 | async-start | bytes 1474560 | tf_op jit(solution)/shard_map/reduce_scatter | solution.py:661
  260.7 13.5 %copy-start.16 = (f32[8,384]{1,0:T(8,128)S(1)}, f32[8,384]{1,0:T(8,128)}, u32[]{:S(2)}) copy-start(f32[8,384]{1,0:T(8,128)} %get-tuple-element.65) | copy-start | bytes 36868
  261.0 13.2 %copy-start.17 = (f32[1,1536]{1,0:T(1,128)S(1)}, f32[1,1536]{1,0:T(1,128)}, u32[]{:S(2)}) copy-start(f32[1,1536]{1,0:T(1,128)} %get-tuple-element.68) | copy-start | bytes 18436
  261.0 13.2 %copy-start.18 = (f32[1,1536]{1,0:T(1,128)S(1)}, f32[1,1536]{1,0:T(1,128)}, u32[]{:S(2)}) copy-start(f32[1,1536]{1,0:T(1,128)} %get-tuple-element.67) | copy-start | bytes 18436
  281.8 301.1 %all-to-all-start.3 = ((bf16[32,32,384]{2,1,0:T(8,128)(2,1)}), bf16[32,32,384]{2,1,0:T(8,128)(2,1)S(1)}, u32[]{:S(2)}, u32[]{:S(2)}) async-start(bf16[32,32,384]{2,1,0:T(8,128)(2,1)} %bitcast.93), calls=%async_computation.3 | async-start | bytes 1572864 | tf_op jit(solution)/shard_map/all_to_all | solution.py:573
  284.6 293.5 %all-reduce.5.cloned.1.call-start = ((), (), s32[]{:S(2)}) async-start(), calls=%async_computation.14 | async-start | bytes 139264 | tf_op jit(solution)/shard_map/psum | solution.py:673
  285.4 361.7 %all-reduce.7.cloned.1.call-start = ((), (), s32[]{:S(2)}) async-start(), calls=%async_computation.25 | async-start | bytes 3538944 | tf_op jit(solution)/shard_map/psum | solution.py:662
  647.0 3.8 copy-start.7
  647.0 3.8 copy-start.8
  647.0 4.9 copy-start.5
  647.0 4.9 copy-start.6
Sparse Core Ops, SparseCore 0:
  10.4 36.4 all-gather.13
  49.3 35.9 all-gather.15
  87.7 29.5 all-gather.17
  119.0 28.6 all-gather.19
  199.1 24.2 reduce-scatter.14
  239.2 23.5 reduce-scatter.12
  266.3 31.3 reduce-scatter.10
  300.7 26.4 reduce-scatter.8
  330.7 28.5 reduce-scatter.18
  362.7 28.5 reduce-scatter.22
  394.2 28.5 reduce-scatter.16
  425.5 28.5 reduce-scatter.20
  460.2 117.8 all-reduce.4
  580.9 66.0 all-reduce.6
